TPU v7x, 32 devices: a whole 2x2x4 slice. The times are simulated.
32 devices in a mesh: section: 4 (over z), seq: 8 (over y, x, core).
Axes of the slice: x: 2, y: 2, z: 4, core: 2. Of those that a mesh axis runs over, the one named last changes fastest.
Arguments:
- bases: int32 [4, 262144], P(None, 'seq'), may hold values from 0 to 3
- stem_weight: bfloat16 [512, 1536], replicated, may hold values from -0.5 to 0.5
- norm_gain: float32 [4, 1536], P('section'), may hold values from 0.25 to 1.75
- conv_taps: float32 [4, 5, 1536], P('section'), may hold values from -2.7 to 2.7
- proj_weight: bfloat16 [4, 1536, 1536], P('section'), may hold values from -0.15625 to 0.15625
- dest: int32 [256], P('seq'), may hold values from 0 to 255, as said below
Outputs:
- hints: bfloat16 [4, 4, 2048, 1536], P('section', None, 'seq')
Inputs may be any that keep to these rules, and one draw needn't show every extreme that they name: dest is a permutation. Slot dest[r] belongs to owner dest[r] // 32; the runs of one index d of seq (r from d * 32) go to every owner in equal numbers, 4 each, and (dest[r] % 32) // 4 equals d.
All inputs are finite; a program needn't handle non-finite values.
Results may differ from a plain program's by a relative error of at most 0.007.
Values may be sent and summed in bfloat16 or wider, within the bound.
A program may use at most 64 MiB of HBM per device.

v0:
```python
import jax
import jax.numpy as jnp
from jax import lax
from jax.sharding import PartitionSpec as P

BLOCK_BP = 128


def extended(block, sides, width):
    for axis, dim in sides:
        count = lax.axis_size(axis)
        forward = [(i, i + 1) for i in range(count - 1)]
        backward = [(target, source) for source, target in forward]
        low = lax.ppermute(
            lax.slice_in_dim(block, block.shape[dim] - width, None, axis=dim), axis, forward
        )
        high = lax.ppermute(lax.slice_in_dim(block, 0, width, axis=dim), axis, backward)
        block = jnp.concatenate([low, block, high], axis=dim)
    return block


def passed_along(value, axis, steps):
    count = lax.axis_size(axis)
    initial, last = (max(0, -steps), min(count, count - steps))
    return lax.ppermute(value, axis, [(source, source + steps) for source in range(initial, last)])


def section_block(current, gain_row, tap_rows, weight):
    wide_state = current.astype(jnp.float32)
    inv_rms = lax.rsqrt(jnp.mean(wide_state * wide_state, axis=-1, keepdims=True) + 1e-06)
    normed = (wide_state * inv_rms * gain_row).astype(jnp.bfloat16)
    reach = tap_rows.shape[0] // 2
    padded = extended(normed, (("seq", 0),), reach)
    length = current.shape[0]
    mixed = jnp.zeros(current.shape, jnp.float32)
    for offset in range(tap_rows.shape[0]):
        mixed = mixed + tap_rows[offset] * padded[offset : offset + length].astype(jnp.float32)
    mixed = mixed.astype(jnp.bfloat16)
    update = jnp.dot(mixed, weight, preferred_element_type=jnp.float32)
    return (wide_state + jax.nn.gelu(update)).astype(jnp.bfloat16)


def on_device(bases, stem_weight, norm_gain, conv_taps, proj_weight, dest):
    micro_count = bases.shape[0]
    row_count = bases.shape[1] // BLOCK_BP
    channels = stem_weight.shape[1]
    section_count = lax.axis_size("section")
    section_id = lax.axis_index("section")
    segs_dev = dest.shape[0]
    per_peer = segs_dev // lax.axis_size("seq")
    seg_rows = row_count // segs_dev
    base_codes = bases.reshape(micro_count * row_count, BLOCK_BP)
    onehot = (base_codes[:, :, None] == jnp.arange(4, dtype=jnp.int32)).astype(jnp.bfloat16)
    onehot = onehot.reshape(micro_count * row_count, BLOCK_BP * 4)
    embedded = jnp.dot(onehot, stem_weight, preferred_element_type=jnp.float32).astype(jnp.bfloat16)
    embedded = embedded.reshape(micro_count, row_count, channels)
    gain_row = norm_gain[0]
    tap_rows = conv_taps[0]
    weight = proj_weight[0]
    send_slot = dest // segs_dev * per_peer + dest % segs_dev % per_peer
    select = (send_slot[None, :] == jnp.arange(segs_dev, dtype=jnp.int32)[:, None]).astype(
        jnp.bfloat16
    )

    def arrange(current):
        grouped = current.reshape(segs_dev, seg_rows * channels)
        ordered = jnp.dot(select, grouped, preferred_element_type=jnp.float32).astype(jnp.bfloat16)
        return ordered.reshape(row_count, channels)

    def advance(moment, carried):
        incoming, hint_rows = carried
        entering = lax.dynamic_index_in_dim(
            embedded, jnp.clip(moment, 0, micro_count - 1), 0, keepdims=False
        )
        current = jnp.where(section_id == 0, entering, incoming)
        leaving = section_block(current, gain_row, tap_rows, weight)
        micro_idx = moment - section_id
        slot_idx = jnp.clip(micro_idx, 0, micro_count - 1)
        in_range = (micro_idx >= 0) & (micro_idx < micro_count)
        arrived = lax.all_to_all(arrange(leaving), "seq", split_axis=0, concat_axis=0, tiled=True)
        previous = lax.dynamic_index_in_dim(hint_rows, slot_idx, 0, keepdims=False)
        arrived = jnp.where(in_range, arrived, previous)
        hint_rows = lax.dynamic_update_index_in_dim(hint_rows, arrived, slot_idx, 0)
        incoming = passed_along(leaving, "section", 1)
        return (incoming, hint_rows)

    start_state = jnp.zeros((row_count, channels), jnp.bfloat16)
    start_hints = jnp.zeros((micro_count, row_count, channels), jnp.bfloat16)
    final_state, hint_rows = lax.fori_loop(
        0, micro_count + section_count - 1, advance, (start_state, start_hints)
    )
    return hint_rows[None]


def solution(mesh):
    return jax.shard_map(
        on_device,
        mesh=mesh,
        in_specs=(
            P(None, "seq"),
            P(),
            P("section", None),
            P("section", None, None),
            P("section", None, None),
            P("seq"),
        ),
        out_specs=P("section", None, "seq", None),
        check_vma=False,
    )
```

profile of v0, /device:TPU:0, one launch (start us, length us, event | category | flops | bytes accessed | tf_op | source)
XLA Modules:
  0.0 320.2 jit_solution(564011685951406488)
XLA Ops:
  3.3 1.9 eq.49
  5.2 3.0 eq.50
  8.2 5.2 %convolution_convert_fusion.1 = bf16[1024,1536]{1,0:T(8,128)(2,1)} fusion(bf16[512,1536]{1,0:T(8,128)(2,1)S(1)} %copy-done, s32[1024,512]{0,1:T(8,128)} %eq.50, s32[512]{0:T(512)S(1)} %eq.52), kind=kOutput, calls=%fused_computation.48 | convolution fusion | flops 1612709888 | bytes 6817792 | tf_op jit(solution)/shard_map/dot_general | solution.py:55
  13.4 1.9 broadcast_in_dim.20
  15.3 304.9 %while.17 = (s32[]{:T(128)}, bf16[256,1536]{1,0:T(8,128)(2,1)S(1)}, bf16[4,256,1536]{2,1,0:T(8,128)(2,1)}, pred[]{:T(512)}, bf16[4,256,1536]{2,1,0:T(8,128)(2,1)...) while((s32[]{:T(128)}, bf16[256,1536]{1,0:T(8,128)(2,1)S(1)}, ...), condition=%wide.region_2.3_spmd.clone, body=%wide.region_0.2_spmd.clone.sunk | while | flops 1252002048 | bytes 23794180 | solution.py:89
  15.3 1.5 fusion.49
  18.4 3.0 collective-permute-start.1
  22.3 5.4 %fusion.52 = bf16[256,1536]{1,0:T(8,128)(2,1)} fusion(bf16[256,1536]{1,0:T(8,128)(2,1)S(1)} %get-tuple-element.323, bf16[1536,1536]{1,0:T(8,128)(2,1)} %get-tuple-element.369, bf16[256,1536]{1,0:T(8,128)(2,1)S(1)} %fusion.50, bf16[2,1536]{1,0:T(2,128)(2,1)S(1)} %collective-permute-done, bf16[2,1536]{1,0:T(2,128)(2,1)S(1)} %collective-permute-done.1, ...), kind=kOutput, calls=%fused_computation.10.clone.1 | convolution fusion | flops 1222901760 | bytes 7120896 | tf_op jit(solution)/shard_map/while/body/eval_jaxpr/dot_general | solution.py:39
  27.7 1.5 reshape.49
  30.7 7.7 %all-to-all-start = ((bf16[8,32,1536]{2,1,0:T(8,128)(2,1)}), bf16[8,32,1536]{2,1,0:T(8,128)(2,1)S(1)}, u32[]{:S(2)}, u32[]{:S(2)}) async-start(bf16[8,32,1536]{2,1,0:T(8,128)(2,1)} %all_to_all.18), calls=%async_computation | async-start | bytes 1572864 | tf_op jit(solution)/shard_map/while/body/eval_jaxpr/all_to_all | solution.py:80
  38.5 3.5 %collective-permute-start.2 = (bf16[256,1536]{1,0:T(8,128)(2,1)}, bf16[256,1536]{1,0:T(8,128)(2,1)S(1)}, u32[]{:S(2)}, u32[]{:S(2)}) collective-permute-start(bf16[256,1536]{1,0:T(8,128)(2,1)} %fusion.52), channel_id=1, source_target_pairs={{0,8},{8,16},{16,24},{1,9},{9,17},{17,25},{2,10},{10,18},{18,26},{... | collective-permute-start | bytes 2359304 | tf_op jit(solution)/shard_map/while/body/eval_jaxpr/ppermute | solution.py:25
  42.0 9.1 %all-to-all-done = bf16[8,32,1536]{2,1,0:T(8,128)(2,1)S(1)} async-done(((bf16[8,32,1536]{2,1,0:T(8,128)(2,1)}), bf16[8,32,1536]{2,1,0:T(8,128)(2,1)S(1)}, u32[]{:S(2)}, u32[]{:S(2)}) %all-to-all-start) | async-done | bytes 786464 | tf_op jit(solution)/shard_map/while/body/eval_jaxpr/all_to_all | solution.py:80
  51.1 2.2 fusion.54
  53.3 6.4 %collective-permute-done.2 = bf16[256,1536]{1,0:T(8,128)(2,1)S(1)} collective-permute-done((bf16[256,1536]{1,0:T(8,128)(2,1)}, bf16[256,1536]{1,0:T(8,128)(2,1)S(1)}, u32[]{:S(2)}, u32[]{:S(2)}) %collective-permute-start.2) | collective-permute-done | bytes 786464 | tf_op jit(solution)/shard_map/while/body/eval_jaxpr/ppermute | solution.py:25
  59.7 1.5 fusion.49
  62.8 3.0 collective-permute-start.1
  66.7 5.4 %fusion.52 = bf16[256,1536]{1,0:T(8,128)(2,1)} fusion(bf16[256,1536]{1,0:T(8,128)(2,1)S(1)} %get-tuple-element.323, bf16[1536,1536]{1,0:T(8,128)(2,1)} %get-tuple-element.369, bf16[256,1536]{1,0:T(8,128)(2,1)S(1)} %fusion.50, bf16[2,1536]{1,0:T(2,128)(2,1)S(1)} %collective-permute-done, bf16[2,1536]{1,0:T(2,128)(2,1)S(1)} %collective-permute-done.1, ...), kind=kOutput, calls=%fused_computation.10.clone.1 | convolution fusion | flops 1222901760 | bytes 7120896 | tf_op jit(solution)/shard_map/while/body/eval_jaxpr/dot_general | solution.py:39
  75.1 5.9 %all-to-all-start = ((bf16[8,32,1536]{2,1,0:T(8,128)(2,1)}), bf16[8,32,1536]{2,1,0:T(8,128)(2,1)S(1)}, u32[]{:S(2)}, u32[]{:S(2)}) async-start(bf16[8,32,1536]{2,1,0:T(8,128)(2,1)} %all_to_all.18), calls=%async_computation | async-start | bytes 1572864 | tf_op jit(solution)/shard_map/while/body/eval_jaxpr/all_to_all | solution.py:80
  81.1 4.3 %collective-permute-start.2 = (bf16[256,1536]{1,0:T(8,128)(2,1)}, bf16[256,1536]{1,0:T(8,128)(2,1)S(1)}, u32[]{:S(2)}, u32[]{:S(2)}) collective-permute-start(bf16[256,1536]{1,0:T(8,128)(2,1)} %fusion.52), channel_id=1, source_target_pairs={{0,8},{8,16},{16,24},{1,9},{9,17},{17,25},{2,10},{10,18},{18,26},{... | collective-permute-start | bytes 2359304 | tf_op jit(solution)/shard_map/while/body/eval_jaxpr/ppermute | solution.py:25
  85.4 8.3 %all-to-all-done = bf16[8,32,1536]{2,1,0:T(8,128)(2,1)S(1)} async-done(((bf16[8,32,1536]{2,1,0:T(8,128)(2,1)}), bf16[8,32,1536]{2,1,0:T(8,128)(2,1)S(1)}, u32[]{:S(2)}, u32[]{:S(2)}) %all-to-all-start) | async-done | bytes 786464 | tf_op jit(solution)/shard_map/while/body/eval_jaxpr/all_to_all | solution.py:80
  93.7 2.2 fusion.54
  95.9 7.2 %collective-permute-done.2 = bf16[256,1536]{1,0:T(8,128)(2,1)S(1)} collective-permute-done((bf16[256,1536]{1,0:T(8,128)(2,1)}, bf16[256,1536]{1,0:T(8,128)(2,1)S(1)}, u32[]{:S(2)}, u32[]{:S(2)}) %collective-permute-start.2) | collective-permute-done | bytes 786464 | tf_op jit(solution)/shard_map/while/body/eval_jaxpr/ppermute | solution.py:25
  103.1 1.5 fusion.49
  106.2 3.0 collective-permute-start.1
  110.1 5.4 %fusion.52 = bf16[256,1536]{1,0:T(8,128)(2,1)} fusion(bf16[256,1536]{1,0:T(8,128)(2,1)S(1)} %get-tuple-element.323, bf16[1536,1536]{1,0:T(8,128)(2,1)} %get-tuple-element.369, bf16[256,1536]{1,0:T(8,128)(2,1)S(1)} %fusion.50, bf16[2,1536]{1,0:T(2,128)(2,1)S(1)} %collective-permute-done, bf16[2,1536]{1,0:T(2,128)(2,1)S(1)} %collective-permute-done.1, ...), kind=kOutput, calls=%fused_computation.10.clone.1 | convolution fusion | flops 1222901760 | bytes 7120896 | tf_op jit(solution)/shard_map/while/body/eval_jaxpr/dot_general | solution.py:39
  115.5 1.5 reshape.49
  118.6 5.9 %all-to-all-start = ((bf16[8,32,1536]{2,1,0:T(8,128)(2,1)}), bf16[8,32,1536]{2,1,0:T(8,128)(2,1)S(1)}, u32[]{:S(2)}, u32[]{:S(2)}) async-start(bf16[8,32,1536]{2,1,0:T(8,128)(2,1)} %all_to_all.18), calls=%async_computation | async-start | bytes 1572864 | tf_op jit(solution)/shard_map/while/body/eval_jaxpr/all_to_all | solution.py:80
  124.5 4.3 %collective-permute-start.2 = (bf16[256,1536]{1,0:T(8,128)(2,1)}, bf16[256,1536]{1,0:T(8,128)(2,1)S(1)}, u32[]{:S(2)}, u32[]{:S(2)}) collective-permute-start(bf16[256,1536]{1,0:T(8,128)(2,1)} %fusion.52), channel_id=1, source_target_pairs={{0,8},{8,16},{16,24},{1,9},{9,17},{17,25},{2,10},{10,18},{18,26},{... | collective-permute-start | bytes 2359304 | tf_op jit(solution)/shard_map/while/body/eval_jaxpr/ppermute | solution.py:25
  128.8 8.3 %all-to-all-done = bf16[8,32,1536]{2,1,0:T(8,128)(2,1)S(1)} async-done(((bf16[8,32,1536]{2,1,0:T(8,128)(2,1)}), bf16[8,32,1536]{2,1,0:T(8,128)(2,1)S(1)}, u32[]{:S(2)}, u32[]{:S(2)}) %all-to-all-start) | async-done | bytes 786464 | tf_op jit(solution)/shard_map/while/body/eval_jaxpr/all_to_all | solution.py:80
  137.1 2.2 fusion.54
  139.3 7.2 %collective-permute-done.2 = bf16[256,1536]{1,0:T(8,128)(2,1)S(1)} collective-permute-done((bf16[256,1536]{1,0:T(8,128)(2,1)}, bf16[256,1536]{1,0:T(8,128)(2,1)S(1)}, u32[]{:S(2)}, u32[]{:S(2)}) %collective-permute-start.2) | collective-permute-done | bytes 786464 | tf_op jit(solution)/shard_map/while/body/eval_jaxpr/ppermute | solution.py:25
  146.6 1.5 fusion.49
  149.7 3.0 collective-permute-start.1
  153.5 5.4 %fusion.52 = bf16[256,1536]{1,0:T(8,128)(2,1)} fusion(bf16[256,1536]{1,0:T(8,128)(2,1)S(1)} %get-tuple-element.323, bf16[1536,1536]{1,0:T(8,128)(2,1)} %get-tuple-element.369, bf16[256,1536]{1,0:T(8,128)(2,1)S(1)} %fusion.50, bf16[2,1536]{1,0:T(2,128)(2,1)S(1)} %collective-permute-done, bf16[2,1536]{1,0:T(2,128)(2,1)S(1)} %collective-permute-done.1, ...), kind=kOutput, calls=%fused_computation.10.clone.1 | convolution fusion | flops 1222901760 | bytes 7120896 | tf_op jit(solution)/shard_map/while/body/eval_jaxpr/dot_general | solution.py:39
  158.9 1.5 reshape.49
  162.0 5.9 %all-to-all-start = ((bf16[8,32,1536]{2,1,0:T(8,128)(2,1)}), bf16[8,32,1536]{2,1,0:T(8,128)(2,1)S(1)}, u32[]{:S(2)}, u32[]{:S(2)}) async-start(bf16[8,32,1536]{2,1,0:T(8,128)(2,1)} %all_to_all.18), calls=%async_computation | async-start | bytes 1572864 | tf_op jit(solution)/shard_map/while/body/eval_jaxpr/all_to_all | solution.py:80
  167.9 4.3 %collective-permute-start.2 = (bf16[256,1536]{1,0:T(8,128)(2,1)}, bf16[256,1536]{1,0:T(8,128)(2,1)S(1)}, u32[]{:S(2)}, u32[]{:S(2)}) collective-permute-start(bf16[256,1536]{1,0:T(8,128)(2,1)} %fusion.52), channel_id=1, source_target_pairs={{0,8},{8,16},{16,24},{1,9},{9,17},{17,25},{2,10},{10,18},{18,26},{... | collective-permute-start | bytes 2359304 | tf_op jit(solution)/shard_map/while/body/eval_jaxpr/ppermute | solution.py:25
  172.3 8.3 %all-to-all-done = bf16[8,32,1536]{2,1,0:T(8,128)(2,1)S(1)} async-done(((bf16[8,32,1536]{2,1,0:T(8,128)(2,1)}), bf16[8,32,1536]{2,1,0:T(8,128)(2,1)S(1)}, u32[]{:S(2)}, u32[]{:S(2)}) %all-to-all-start) | async-done | bytes 786464 | tf_op jit(solution)/shard_map/while/body/eval_jaxpr/all_to_all | solution.py:80
  180.5 2.2 fusion.54
  182.7 7.2 %collective-permute-done.2 = bf16[256,1536]{1,0:T(8,128)(2,1)S(1)} collective-permute-done((bf16[256,1536]{1,0:T(8,128)(2,1)}, bf16[256,1536]{1,0:T(8,128)(2,1)S(1)}, u32[]{:S(2)}, u32[]{:S(2)}) %collective-permute-start.2) | collective-permute-done | bytes 786464 | tf_op jit(solution)/shard_map/while/body/eval_jaxpr/ppermute | solution.py:25
  190.0 1.5 fusion.49
  193.1 3.0 collective-permute-start.1
  196.9 5.4 %fusion.52 = bf16[256,1536]{1,0:T(8,128)(2,1)} fusion(bf16[256,1536]{1,0:T(8,128)(2,1)S(1)} %get-tuple-element.323, bf16[1536,1536]{1,0:T(8,128)(2,1)} %get-tuple-element.369, bf16[256,1536]{1,0:T(8,128)(2,1)S(1)} %fusion.50, bf16[2,1536]{1,0:T(2,128)(2,1)S(1)} %collective-permute-done, bf16[2,1536]{1,0:T(2,128)(2,1)S(1)} %collective-permute-done.1, ...), kind=kOutput, calls=%fused_computation.10.clone.1 | convolution fusion | flops 1222901760 | bytes 7120896 | tf_op jit(solution)/shard_map/while/body/eval_jaxpr/dot_general | solution.py:39
  205.4 5.9 %all-to-all-start = ((bf16[8,32,1536]{2,1,0:T(8,128)(2,1)}), bf16[8,32,1536]{2,1,0:T(8,128)(2,1)S(1)}, u32[]{:S(2)}, u32[]{:S(2)}) async-start(bf16[8,32,1536]{2,1,0:T(8,128)(2,1)} %all_to_all.18), calls=%async_computation | async-start | bytes 1572864 | tf_op jit(solution)/shard_map/while/body/eval_jaxpr/all_to_all | solution.py:80
  211.3 4.3 %collective-permute-start.2 = (bf16[256,1536]{1,0:T(8,128)(2,1)}, bf16[256,1536]{1,0:T(8,128)(2,1)S(1)}, u32[]{:S(2)}, u32[]{:S(2)}) collective-permute-start(bf16[256,1536]{1,0:T(8,128)(2,1)} %fusion.52), channel_id=1, source_target_pairs={{0,8},{8,16},{16,24},{1,9},{9,17},{17,25},{2,10},{10,18},{18,26},{... | collective-permute-start | bytes 2359304 | tf_op jit(solution)/shard_map/while/body/eval_jaxpr/ppermute | solution.py:25
  215.7 8.3 %all-to-all-done = bf16[8,32,1536]{2,1,0:T(8,128)(2,1)S(1)} async-done(((bf16[8,32,1536]{2,1,0:T(8,128)(2,1)}), bf16[8,32,1536]{2,1,0:T(8,128)(2,1)S(1)}, u32[]{:S(2)}, u32[]{:S(2)}) %all-to-all-start) | async-done | bytes 786464 | tf_op jit(solution)/shard_map/while/body/eval_jaxpr/all_to_all | solution.py:80
  224.0 2.2 fusion.54
  226.1 7.2 %collective-permute-done.2 = bf16[256,1536]{1,0:T(8,128)(2,1)S(1)} collective-permute-done((bf16[256,1536]{1,0:T(8,128)(2,1)}, bf16[256,1536]{1,0:T(8,128)(2,1)S(1)}, u32[]{:S(2)}, u32[]{:S(2)}) %collective-permute-start.2) | collective-permute-done | bytes 786464 | tf_op jit(solution)/shard_map/while/body/eval_jaxpr/ppermute | solution.py:25
  233.4 1.5 fusion.49
  236.5 3.0 collective-permute-start.1
  240.3 5.4 %fusion.52 = bf16[256,1536]{1,0:T(8,128)(2,1)} fusion(bf16[256,1536]{1,0:T(8,128)(2,1)S(1)} %get-tuple-element.323, bf16[1536,1536]{1,0:T(8,128)(2,1)} %get-tuple-element.369, bf16[256,1536]{1,0:T(8,128)(2,1)S(1)} %fusion.50, bf16[2,1536]{1,0:T(2,128)(2,1)S(1)} %collective-permute-done, bf16[2,1536]{1,0:T(2,128)(2,1)S(1)} %collective-permute-done.1, ...), kind=kOutput, calls=%fused_computation.10.clone.1 | convolution fusion | flops 1222901760 | bytes 7120896 | tf_op jit(solution)/shard_map/while/body/eval_jaxpr/dot_general | solution.py:39
  248.8 5.9 %all-to-all-start = ((bf16[8,32,1536]{2,1,0:T(8,128)(2,1)}), bf16[8,32,1536]{2,1,0:T(8,128)(2,1)S(1)}, u32[]{:S(2)}, u32[]{:S(2)}) async-start(bf16[8,32,1536]{2,1,0:T(8,128)(2,1)} %all_to_all.18), calls=%async_computation | async-start | bytes 1572864 | tf_op jit(solution)/shard_map/while/body/eval_jaxpr/all_to_all | solution.py:80
  254.8 4.3 %collective-permute-start.2 = (bf16[256,1536]{1,0:T(8,128)(2,1)}, bf16[256,1536]{1,0:T(8,128)(2,1)S(1)}, u32[]{:S(2)}, u32[]{:S(2)}) collective-permute-start(bf16[256,1536]{1,0:T(8,128)(2,1)} %fusion.52), channel_id=1, source_target_pairs={{0,8},{8,16},{16,24},{1,9},{9,17},{17,25},{2,10},{10,18},{18,26},{... | collective-permute-start | bytes 2359304 | tf_op jit(solution)/shard_map/while/body/eval_jaxpr/ppermute | solution.py:25
  259.1 8.3 %all-to-all-done = bf16[8,32,1536]{2,1,0:T(8,128)(2,1)S(1)} async-done(((bf16[8,32,1536]{2,1,0:T(8,128)(2,1)}), bf16[8,32,1536]{2,1,0:T(8,128)(2,1)S(1)}, u32[]{:S(2)}, u32[]{:S(2)}) %all-to-all-start) | async-done | bytes 786464 | tf_op jit(solution)/shard_map/while/body/eval_jaxpr/all_to_all | solution.py:80
  267.4 2.2 fusion.54
  269.6 7.2 %collective-permute-done.2 = bf16[256,1536]{1,0:T(8,128)(2,1)S(1)} collective-permute-done((bf16[256,1536]{1,0:T(8,128)(2,1)}, bf16[256,1536]{1,0:T(8,128)(2,1)S(1)}, u32[]{:S(2)}, u32[]{:S(2)}) %collective-permute-start.2) | collective-permute-done | bytes 786464 | tf_op jit(solution)/shard_map/while/body/eval_jaxpr/ppermute | solution.py:25
  276.8 1.5 fusion.49
  279.9 3.0 collective-permute-start.1
  283.8 5.4 %fusion.52 = bf16[256,1536]{1,0:T(8,128)(2,1)} fusion(bf16[256,1536]{1,0:T(8,128)(2,1)S(1)} %get-tuple-element.323, bf16[1536,1536]{1,0:T(8,128)(2,1)} %get-tuple-element.369, bf16[256,1536]{1,0:T(8,128)(2,1)S(1)} %fusion.50, bf16[2,1536]{1,0:T(2,128)(2,1)S(1)} %collective-permute-done, bf16[2,1536]{1,0:T(2,128)(2,1)S(1)} %collective-permute-done.1, ...), kind=kOutput, calls=%fused_computation.10.clone.1 | convolution fusion | flops 1222901760 | bytes 7120896 | tf_op jit(solution)/shard_map/while/body/eval_jaxpr/dot_general | solution.py:39
  292.2 5.9 %all-to-all-start = ((bf16[8,32,1536]{2,1,0:T(8,128)(2,1)}), bf16[8,32,1536]{2,1,0:T(8,128)(2,1)S(1)}, u32[]{:S(2)}, u32[]{:S(2)}) async-start(bf16[8,32,1536]{2,1,0:T(8,128)(2,1)} %all_to_all.18), calls=%async_computation | async-start | bytes 1572864 | tf_op jit(solution)/shard_map/while/body/eval_jaxpr/all_to_all | solution.py:80
  298.2 4.3 %collective-permute-start.2 = (bf16[256,1536]{1,0:T(8,128)(2,1)}, bf16[256,1536]{1,0:T(8,128)(2,1)S(1)}, u32[]{:S(2)}, u32[]{:S(2)}) collective-permute-start(bf16[256,1536]{1,0:T(8,128)(2,1)} %fusion.52), channel_id=1, source_target_pairs={{0,8},{8,16},{16,24},{1,9},{9,17},{17,25},{2,10},{10,18},{18,26},{... | collective-permute-start | bytes 2359304 | tf_op jit(solution)/shard_map/while/body/eval_jaxpr/ppermute | solution.py:25
  302.5 8.3 %all-to-all-done = bf16[8,32,1536]{2,1,0:T(8,128)(2,1)S(1)} async-done(((bf16[8,32,1536]{2,1,0:T(8,128)(2,1)}), bf16[8,32,1536]{2,1,0:T(8,128)(2,1)S(1)}, u32[]{:S(2)}, u32[]{:S(2)}) %all-to-all-start) | async-done | bytes 786464 | tf_op jit(solution)/shard_map/while/body/eval_jaxpr/all_to_all | solution.py:80
  310.8 2.2 fusion.54
  313.0 7.2 %collective-permute-done.2 = bf16[256,1536]{1,0:T(8,128)(2,1)S(1)} collective-permute-done((bf16[256,1536]{1,0:T(8,128)(2,1)}, bf16[256,1536]{1,0:T(8,128)(2,1)S(1)}, u32[]{:S(2)}, u32[]{:S(2)}) %collective-permute-start.2) | collective-permute-done | bytes 786464 | tf_op jit(solution)/shard_map/while/body/eval_jaxpr/ppermute | solution.py:25
  (85 shorter events, 36.9 us)
Async XLA Ops:
  0.0 8.2 %copy-start = (bf16[512,1536]{1,0:T(8,128)(2,1)S(1)}, bf16[512,1536]{1,0:T(8,128)(2,1)}, u32[]{:S(2)}) copy-start(bf16[512,1536]{1,0:T(8,128)(2,1)} %param.9) | copy-start | bytes 4718596
  13.4 1.9 copy-start.1
  17.1 4.4 %collective-permute-start = (bf16[2,1536]{1,0:T(2,128)(2,1)S(1)}, bf16[2,1536]{1,0:T(2,128)(2,1)S(1)}, u32[]{:S(2)}, u32[]{:S(2)}) collective-permute-start(bf16[2,1536]{1,0:T(2,128)(2,1)S(1)} %get-tuple-element.325), channel_id=1, source_target_pairs={{1,0},{2,1},{3,2},{4,3},{5,4},{6,5},{7,6},{9,8},{10,9},{11,10},{12... | collective-permute-start | bytes 18440 | tf_op jit(solution)/shard_map/while/body/eval_jaxpr/ppermute | solution.py:17
  18.4 3.8 %collective-permute-start.1 = (bf16[2,1536]{1,0:T(2,128)(2,1)S(1)}, bf16[2,1536]{1,0:T(2,128)(2,1)S(1)}, u32[]{:S(2)}, u32[]{:S(2)}) collective-permute-start(bf16[2,1536]{1,0:T(2,128)(2,1)S(1)} %get-tuple-element.326), channel_id=1, source_target_pairs={{0,1},{1,2},{2,3},{3,4},{4,5},{5,6},{6,7},{8,9},{9,10},{10,11},{11... | collective-permute-start | bytes 18440 | tf_op jit(solution)/shard_map/while/body/eval_jaxpr/ppermute | solution.py:14
  30.7 20.3 %all-to-all-start = ((bf16[8,32,1536]{2,1,0:T(8,128)(2,1)}), bf16[8,32,1536]{2,1,0:T(8,128)(2,1)S(1)}, u32[]{:S(2)}, u32[]{:S(2)}) async-start(bf16[8,32,1536]{2,1,0:T(8,128)(2,1)} %all_to_all.18), calls=%async_computation | async-start | bytes 1572864 | tf_op jit(solution)/shard_map/while/body/eval_jaxpr/all_to_all | solution.py:80
  38.5 21.2 %collective-permute-start.2 = (bf16[256,1536]{1,0:T(8,128)(2,1)}, bf16[256,1536]{1,0:T(8,128)(2,1)S(1)}, u32[]{:S(2)}, u32[]{:S(2)}) collective-permute-start(bf16[256,1536]{1,0:T(8,128)(2,1)} %fusion.52), channel_id=1, source_target_pairs={{0,8},{8,16},{16,24},{1,9},{9,17},{17,25},{2,10},{10,18},{18,26},{... | collective-permute-start | bytes 2359304 | tf_op jit(solution)/shard_map/while/body/eval_jaxpr/ppermute | solution.py:25
  61.5 4.4 %collective-permute-start = (bf16[2,1536]{1,0:T(2,128)(2,1)S(1)}, bf16[2,1536]{1,0:T(2,128)(2,1)S(1)}, u32[]{:S(2)}, u32[]{:S(2)}) collective-permute-start(bf16[2,1536]{1,0:T(2,128)(2,1)S(1)} %get-tuple-element.325), channel_id=1, source_target_pairs={{1,0},{2,1},{3,2},{4,3},{5,4},{6,5},{7,6},{9,8},{10,9},{11,10},{12... | collective-permute-start | bytes 18440 | tf_op jit(solution)/shard_map/while/body/eval_jaxpr/ppermute | solution.py:17
  62.8 3.8 %collective-permute-start.1 = (bf16[2,1536]{1,0:T(2,128)(2,1)S(1)}, bf16[2,1536]{1,0:T(2,128)(2,1)S(1)}, u32[]{:S(2)}, u32[]{:S(2)}) collective-permute-start(bf16[2,1536]{1,0:T(2,128)(2,1)S(1)} %get-tuple-element.326), channel_id=1, source_target_pairs={{0,1},{1,2},{2,3},{3,4},{4,5},{5,6},{6,7},{8,9},{9,10},{10,11},{11... | collective-permute-start | bytes 18440 | tf_op jit(solution)/shard_map/while/body/eval_jaxpr/ppermute | solution.py:14
  75.1 18.6 %all-to-all-start = ((bf16[8,32,1536]{2,1,0:T(8,128)(2,1)}), bf16[8,32,1536]{2,1,0:T(8,128)(2,1)S(1)}, u32[]{:S(2)}, u32[]{:S(2)}) async-start(bf16[8,32,1536]{2,1,0:T(8,128)(2,1)} %all_to_all.18), calls=%async_computation | async-start | bytes 1572864 | tf_op jit(solution)/shard_map/while/body/eval_jaxpr/all_to_all | solution.py:80
  81.1 22.0 %collective-permute-start.2 = (bf16[256,1536]{1,0:T(8,128)(2,1)}, bf16[256,1536]{1,0:T(8,128)(2,1)S(1)}, u32[]{:S(2)}, u32[]{:S(2)}) collective-permute-start(bf16[256,1536]{1,0:T(8,128)(2,1)} %fusion.52), channel_id=1, source_target_pairs={{0,8},{8,16},{16,24},{1,9},{9,17},{17,25},{2,10},{10,18},{18,26},{... | collective-permute-start | bytes 2359304 | tf_op jit(solution)/shard_map/while/body/eval_jaxpr/ppermute | solution.py:25
  104.9 4.4 %collective-permute-start = (bf16[2,1536]{1,0:T(2,128)(2,1)S(1)}, bf16[2,1536]{1,0:T(2,128)(2,1)S(1)}, u32[]{:S(2)}, u32[]{:S(2)}) collective-permute-start(bf16[2,1536]{1,0:T(2,128)(2,1)S(1)} %get-tuple-element.325), channel_id=1, source_target_pairs={{1,0},{2,1},{3,2},{4,3},{5,4},{6,5},{7,6},{9,8},{10,9},{11,10},{12... | collective-permute-start | bytes 18440 | tf_op jit(solution)/shard_map/while/body/eval_jaxpr/ppermute | solution.py:17
  106.2 3.8 %collective-permute-start.1 = (bf16[2,1536]{1,0:T(2,128)(2,1)S(1)}, bf16[2,1536]{1,0:T(2,128)(2,1)S(1)}, u32[]{:S(2)}, u32[]{:S(2)}) collective-permute-start(bf16[2,1536]{1,0:T(2,128)(2,1)S(1)} %get-tuple-element.326), channel_id=1, source_target_pairs={{0,1},{1,2},{2,3},{3,4},{4,5},{5,6},{6,7},{8,9},{9,10},{10,11},{11... | collective-permute-start | bytes 18440 | tf_op jit(solution)/shard_map/while/body/eval_jaxpr/ppermute | solution.py:14
  118.6 18.6 %all-to-all-start = ((bf16[8,32,1536]{2,1,0:T(8,128)(2,1)}), bf16[8,32,1536]{2,1,0:T(8,128)(2,1)S(1)}, u32[]{:S(2)}, u32[]{:S(2)}) async-start(bf16[8,32,1536]{2,1,0:T(8,128)(2,1)} %all_to_all.18), calls=%async_computation | async-start | bytes 1572864 | tf_op jit(solution)/shard_map/while/body/eval_jaxpr/all_to_all | solution.py:80
  124.5 22.0 %collective-permute-start.2 = (bf16[256,1536]{1,0:T(8,128)(2,1)}, bf16[256,1536]{1,0:T(8,128)(2,1)S(1)}, u32[]{:S(2)}, u32[]{:S(2)}) collective-permute-start(bf16[256,1536]{1,0:T(8,128)(2,1)} %fusion.52), channel_id=1, source_target_pairs={{0,8},{8,16},{16,24},{1,9},{9,17},{17,25},{2,10},{10,18},{18,26},{... | collective-permute-start | bytes 2359304 | tf_op jit(solution)/shard_map/while/body/eval_jaxpr/ppermute | solution.py:25
  148.4 4.4 %collective-permute-start = (bf16[2,1536]{1,0:T(2,128)(2,1)S(1)}, bf16[2,1536]{1,0:T(2,128)(2,1)S(1)}, u32[]{:S(2)}, u32[]{:S(2)}) collective-permute-start(bf16[2,1536]{1,0:T(2,128)(2,1)S(1)} %get-tuple-element.325), channel_id=1, source_target_pairs={{1,0},{2,1},{3,2},{4,3},{5,4},{6,5},{7,6},{9,8},{10,9},{11,10},{12... | collective-permute-start | bytes 18440 | tf_op jit(solution)/shard_map/while/body/eval_jaxpr/ppermute | solution.py:17
  149.7 3.8 %collective-permute-start.1 = (bf16[2,1536]{1,0:T(2,128)(2,1)S(1)}, bf16[2,1536]{1,0:T(2,128)(2,1)S(1)}, u32[]{:S(2)}, u32[]{:S(2)}) collective-permute-start(bf16[2,1536]{1,0:T(2,128)(2,1)S(1)} %get-tuple-element.326), channel_id=1, source_target_pairs={{0,1},{1,2},{2,3},{3,4},{4,5},{5,6},{6,7},{8,9},{9,10},{10,11},{11... | collective-permute-start | bytes 18440 | tf_op jit(solution)/shard_map/while/body/eval_jaxpr/ppermute | solution.py:14
  162.0 18.6 %all-to-all-start = ((bf16[8,32,1536]{2,1,0:T(8,128)(2,1)}), bf16[8,32,1536]{2,1,0:T(8,128)(2,1)S(1)}, u32[]{:S(2)}, u32[]{:S(2)}) async-start(bf16[8,32,1536]{2,1,0:T(8,128)(2,1)} %all_to_all.18), calls=%async_computation | async-start | bytes 1572864 | tf_op jit(solution)/shard_map/while/body/eval_jaxpr/all_to_all | solution.py:80
  167.9 22.0 %collective-permute-start.2 = (bf16[256,1536]{1,0:T(8,128)(2,1)}, bf16[256,1536]{1,0:T(8,128)(2,1)S(1)}, u32[]{:S(2)}, u32[]{:S(2)}) collective-permute-start(bf16[256,1536]{1,0:T(8,128)(2,1)} %fusion.52), channel_id=1, source_target_pairs={{0,8},{8,16},{16,24},{1,9},{9,17},{17,25},{2,10},{10,18},{18,26},{... | collective-permute-start | bytes 2359304 | tf_op jit(solution)/shard_map/while/body/eval_jaxpr/ppermute | solution.py:25
  191.8 4.4 %collective-permute-start = (bf16[2,1536]{1,0:T(2,128)(2,1)S(1)}, bf16[2,1536]{1,0:T(2,128)(2,1)S(1)}, u32[]{:S(2)}, u32[]{:S(2)}) collective-permute-start(bf16[2,1536]{1,0:T(2,128)(2,1)S(1)} %get-tuple-element.325), channel_id=1, source_target_pairs={{1,0},{2,1},{3,2},{4,3},{5,4},{6,5},{7,6},{9,8},{10,9},{11,10},{12... | collective-permute-start | bytes 18440 | tf_op jit(solution)/shard_map/while/body/eval_jaxpr/ppermute | solution.py:17
  193.1 3.8 %collective-permute-start.1 = (bf16[2,1536]{1,0:T(2,128)(2,1)S(1)}, bf16[2,1536]{1,0:T(2,128)(2,1)S(1)}, u32[]{:S(2)}, u32[]{:S(2)}) collective-permute-start(bf16[2,1536]{1,0:T(2,128)(2,1)S(1)} %get-tuple-element.326), channel_id=1, source_target_pairs={{0,1},{1,2},{2,3},{3,4},{4,5},{5,6},{6,7},{8,9},{9,10},{10,11},{11... | collective-permute-start | bytes 18440 | tf_op jit(solution)/shard_map/while/body/eval_jaxpr/ppermute | solution.py:14
  205.4 18.6 %all-to-all-start = ((bf16[8,32,1536]{2,1,0:T(8,128)(2,1)}), bf16[8,32,1536]{2,1,0:T(8,128)(2,1)S(1)}, u32[]{:S(2)}, u32[]{:S(2)}) async-start(bf16[8,32,1536]{2,1,0:T(8,128)(2,1)} %all_to_all.18), calls=%async_computation | async-start | bytes 1572864 | tf_op jit(solution)/shard_map/while/body/eval_jaxpr/all_to_all | solution.py:80
  211.3 22.0 %collective-permute-start.2 = (bf16[256,1536]{1,0:T(8,128)(2,1)}, bf16[256,1536]{1,0:T(8,128)(2,1)S(1)}, u32[]{:S(2)}, u32[]{:S(2)}) collective-permute-start(bf16[256,1536]{1,0:T(8,128)(2,1)} %fusion.52), channel_id=1, source_target_pairs={{0,8},{8,16},{16,24},{1,9},{9,17},{17,25},{2,10},{10,18},{18,26},{... | collective-permute-start | bytes 2359304 | tf_op jit(solution)/shard_map/while/body/eval_jaxpr/ppermute | solution.py:25
  235.2 4.4 %collective-permute-start = (bf16[2,1536]{1,0:T(2,128)(2,1)S(1)}, bf16[2,1536]{1,0:T(2,128)(2,1)S(1)}, u32[]{:S(2)}, u32[]{:S(2)}) collective-permute-start(bf16[2,1536]{1,0:T(2,128)(2,1)S(1)} %get-tuple-element.325), channel_id=1, source_target_pairs={{1,0},{2,1},{3,2},{4,3},{5,4},{6,5},{7,6},{9,8},{10,9},{11,10},{12... | collective-permute-start | bytes 18440 | tf_op jit(solution)/shard_map/while/body/eval_jaxpr/ppermute | solution.py:17
  236.5 3.8 %collective-permute-start.1 = (bf16[2,1536]{1,0:T(2,128)(2,1)S(1)}, bf16[2,1536]{1,0:T(2,128)(2,1)S(1)}, u32[]{:S(2)}, u32[]{:S(2)}) collective-permute-start(bf16[2,1536]{1,0:T(2,128)(2,1)S(1)} %get-tuple-element.326), channel_id=1, source_target_pairs={{0,1},{1,2},{2,3},{3,4},{4,5},{5,6},{6,7},{8,9},{9,10},{10,11},{11... | collective-permute-start | bytes 18440 | tf_op jit(solution)/shard_map/while/body/eval_jaxpr/ppermute | solution.py:14
  248.8 18.6 %all-to-all-start = ((bf16[8,32,1536]{2,1,0:T(8,128)(2,1)}), bf16[8,32,1536]{2,1,0:T(8,128)(2,1)S(1)}, u32[]{:S(2)}, u32[]{:S(2)}) async-start(bf16[8,32,1536]{2,1,0:T(8,128)(2,1)} %all_to_all.18), calls=%async_computation | async-start | bytes 1572864 | tf_op jit(solution)/shard_map/while/body/eval_jaxpr/all_to_all | solution.py:80
  254.8 22.0 %collective-permute-start.2 = (bf16[256,1536]{1,0:T(8,128)(2,1)}, bf16[256,1536]{1,0:T(8,128)(2,1)S(1)}, u32[]{:S(2)}, u32[]{:S(2)}) collective-permute-start(bf16[256,1536]{1,0:T(8,128)(2,1)} %fusion.52), channel_id=1, source_target_pairs={{0,8},{8,16},{16,24},{1,9},{9,17},{17,25},{2,10},{10,18},{18,26},{... | collective-permute-start | bytes 2359304 | tf_op jit(solution)/shard_map/while/body/eval_jaxpr/ppermute | solution.py:25
  278.6 4.4 %collective-permute-start = (bf16[2,1536]{1,0:T(2,128)(2,1)S(1)}, bf16[2,1536]{1,0:T(2,128)(2,1)S(1)}, u32[]{:S(2)}, u32[]{:S(2)}) collective-permute-start(bf16[2,1536]{1,0:T(2,128)(2,1)S(1)} %get-tuple-element.325), channel_id=1, source_target_pairs={{1,0},{2,1},{3,2},{4,3},{5,4},{6,5},{7,6},{9,8},{10,9},{11,10},{12... | collective-permute-start | bytes 18440 | tf_op jit(solution)/shard_map/while/body/eval_jaxpr/ppermute | solution.py:17
  279.9 3.8 %collective-permute-start.1 = (bf16[2,1536]{1,0:T(2,128)(2,1)S(1)}, bf16[2,1536]{1,0:T(2,128)(2,1)S(1)}, u32[]{:S(2)}, u32[]{:S(2)}) collective-permute-start(bf16[2,1536]{1,0:T(2,128)(2,1)S(1)} %get-tuple-element.326), channel_id=1, source_target_pairs={{0,1},{1,2},{2,3},{3,4},{4,5},{5,6},{6,7},{8,9},{9,10},{10,11},{11... | collective-permute-start | bytes 18440 | tf_op jit(solution)/shard_map/while/body/eval_jaxpr/ppermute | solution.py:14
  292.2 18.6 %all-to-all-start = ((bf16[8,32,1536]{2,1,0:T(8,128)(2,1)}), bf16[8,32,1536]{2,1,0:T(8,128)(2,1)S(1)}, u32[]{:S(2)}, u32[]{:S(2)}) async-start(bf16[8,32,1536]{2,1,0:T(8,128)(2,1)} %all_to_all.18), calls=%async_computation | async-start | bytes 1572864 | tf_op jit(solution)/shard_map/while/body/eval_jaxpr/all_to_all | solution.py:80
  298.2 22.0 %collective-permute-start.2 = (bf16[256,1536]{1,0:T(8,128)(2,1)}, bf16[256,1536]{1,0:T(8,128)(2,1)S(1)}, u32[]{:S(2)}, u32[]{:S(2)}) collective-permute-start(bf16[256,1536]{1,0:T(8,128)(2,1)} %fusion.52), channel_id=1, source_target_pairs={{0,8},{8,16},{16,24},{1,9},{9,17},{17,25},{2,10},{10,18},{18,26},{... | collective-permute-start | bytes 2359304 | tf_op jit(solution)/shard_map/while/body/eval_jaxpr/ppermute | solution.py:25
where the time goes:
time: 322 us; the launch traced here: 320 us
  waiting for transfers between devices  114 us (35%)
  starting transfers between devices  103 us (32%)
  matrix products  45.4 us (14%)
  local copies, waits for them, and re-layouts  29 us (9%)
  other arithmetic  28.6 us (9%)
    all_to_all x7, waiting for transfers between devices, advance(): lax.all_to_all(arrange(leaving), 'seq', split_axis=0, concat_axis=0, tile...  58.7 us
    ppermute x7, waiting for transfers between devices, passed_along(): lax.ppermute(value, axis, [(source, source + steps) for source in range(i...  49.9 us
    all_to_all x7, starting transfers between devices, advance(): lax.all_to_all(arrange(leaving), 'seq', split_axis=0, concat_axis=0, tile...  43.4 us
    dot_general x7, matrix products, section_block(): update = jnp.dot(mixed, weight, preferred_element_type=jnp.float32)  37.8 us
    ppermute x7, starting transfers between devices, passed_along(): lax.ppermute(value, axis, [(source, source + steps) for source in range(i...  29.4 us
    ppermute x7, starting transfers between devices, extended(): lax.ppermute(lax.slice_in_dim(block, block.shape[dim] - width, None, axis...  21.2 us
    dynamic_update_slice x7, other arithmetic, advance(): hint_rows = lax.dynamic_update_index_in_dim(hint_rows, arrived, slot_idx, 0)  15.4 us
    reduce_sum x7, other arithmetic, section_block(): jnp.mean(wide_state * wide_state, axis=-1, keepdims=True) + 1e-06  10.4 us
  transfers between devices with their start and end apart: 28, of which 21 were waited for; matrix products, arithmetic and copies ran while one was open for 5% of the time, Pallas kernels for 0%

commit v1 on v0

--- a/solution.py
+++ b/solution.py
@@ -4,6 +4,22 @@
 from jax.sharding import PartitionSpec as P
 
 BLOCK_BP = 128
+
+
+def pairwise_exchange(x, axis, split, join):
+    ways, here = (lax.axis_size(axis), lax.axis_index(axis))
+    width = x.shape[split] // ways
+    dims = list(x.shape)
+    dims[split] = width
+    height = dims[join]
+    dims[join] = height * ways
+    full = jnp.zeros(dims, x.dtype)
+    for mask in range(ways):
+        part = lax.dynamic_slice_in_dim(x, (here ^ mask) * width, width, axis=split)
+        if mask:
+            part = lax.ppermute(part, axis, [(d, d ^ mask) for d in range(ways)])
+        full = lax.dynamic_update_slice_in_dim(full, part, (here ^ mask) * height, axis=join)
+    return full
 
 
 def extended(block, sides, width):
@@ -77,7 +93,7 @@
         micro_idx = moment - section_id
         slot_idx = jnp.clip(micro_idx, 0, micro_count - 1)
         in_range = (micro_idx >= 0) & (micro_idx < micro_count)
-        arrived = lax.all_to_all(arrange(leaving), "seq", split_axis=0, concat_axis=0, tiled=True)
+        arrived = pairwise_exchange(arrange(leaving), "seq", 0, 0)
         previous = lax.dynamic_index_in_dim(hint_rows, slot_idx, 0, keepdims=False)
         arrived = jnp.where(in_range, arrived, previous)
         hint_rows = lax.dynamic_update_index_in_dim(hint_rows, arrived, slot_idx, 0)

time: 322 us -> 311 us (0.966)
  waiting for transfers between devices: 114 us -> 31.6 us
  starting transfers between devices: 103 us -> 155 us
  local copies, waits for them, and re-layouts: 29 us -> 52.3 us
  other arithmetic: 28.6 us -> 20.7 us
    ppermute x0 -> x49, starting transfers between devices: none -> 87.1 us  [pairwise_exchange(): part = lax.ppermute(part, axis, [(d, d ^ mask) for d in range(ways)])]
    all_to_all x7 -> x0, waiting for transfers between devices: 58.7 us -> none  [advance(): lax.all_to_all(arrange(leaving), 'seq', split_axis=0, concat_axis=0, tile...]
    ppermute x7, waiting for transfers between devices: 49.9 us -> 0.42 us  [passed_along(): lax.ppermute(value, axis, [(source, source + steps) for source in range(i...]
    all_to_all x7 -> x0, starting transfers between devices: 43.4 us -> none  [advance(): lax.all_to_all(arrange(leaving), 'seq', split_axis=0, concat_axis=0, tile...]
    ppermute x0 -> x49, waiting for transfers between devices: none -> 31.1 us  [pairwise_exchange(): part = lax.ppermute(part, axis, [(d, d ^ mask) for d in range(ways)])]
    dynamic_slice x0 -> x14, local copies, waits for them, and re-layouts: none -> 13.6 us  [the longest x7 8.29 us: advance(): previous = lax.dynamic_index_in_dim(hint_rows, slot_idx, 0, keepdims=False)]
    all_to_all x7 -> x0, local copies, waits for them, and re-layouts: 8.67 us -> none  [advance(): lax.all_to_all(arrange(leaving), 'seq', split_axis=0, concat_axis=0, tile...]
    ppermute x7, starting transfers between devices: 29.4 us -> 37.7 us  [passed_along(): lax.ppermute(value, axis, [(source, source + steps) for source in range(i...]
  transfers between devices with their start and end apart: 28 -> 70, of which waited for: 21 -> 8; matrix products, arithmetic and copies ran while one was open for 5% -> 10% of each run, Pallas kernels for 0% -> 0%
where the time goes in v1:
time: 311 us; the launch traced here: 307 us
  starting transfers between devices  155 us (50%)
  local copies, waits for them, and re-layouts  52.3 us (17%)
  matrix products  45.4 us (15%)
  waiting for transfers between devices  31.6 us (10%)
  other arithmetic  20.7 us (7%)
    ppermute x49, starting transfers between devices, pairwise_exchange(): part = lax.ppermute(part, axis, [(d, d ^ mask) for d in range(ways)])  87.1 us
    dot_general x7, matrix products, section_block(): update = jnp.dot(mixed, weight, preferred_element_type=jnp.float32)  37.8 us
    ppermute x7, starting transfers between devices, passed_along(): lax.ppermute(value, axis, [(source, source + steps) for source in range(i...  37.7 us
    ppermute x49, waiting for transfers between devices, pairwise_exchange(): part = lax.ppermute(part, axis, [(d, d ^ mask) for d in range(ways)])  31.1 us
    ppermute x7, starting transfers between devices, extended(): lax.ppermute(lax.slice_in_dim(block, block.shape[dim] - width, None, axis...  21.2 us
    reduce_sum x7, other arithmetic, section_block(): jnp.mean(wide_state * wide_state, axis=-1, keepdims=True) + 1e-06  10.5 us
    reshape x7, local copies, waits for them, and re-layouts, arrange(): grouped = current.reshape(segs_dev, seg_rows * channels)  10.3 us
    ppermute x7, starting transfers between devices, extended(): lax.ppermute(lax.slice_in_dim(block, 0, width, axis=dim), axis, backward)  9.04 us
  transfers between devices with their start and end apart: 70, of which 8 were waited for; matrix products, arithmetic and copies ran while one was open for 10% of the time, Pallas kernels for 0%

profile of v1, /device:TPU:0, one launch (start us, length us, event | category | flops | bytes accessed | tf_op | source)
XLA Modules:
  0.0 306.6 jit_solution(3524165156307571791)
XLA Ops:
  3.9 1.9 eq.49
  5.8 3.0 eq.50
  8.8 5.2 %convolution_convert_fusion.1 = bf16[1024,1536]{1,0:T(8,128)(2,1)} fusion(bf16[512,1536]{1,0:T(8,128)(2,1)S(1)} %copy-done, s32[1024,512]{0,1:T(8,128)} %eq.50, s32[512]{0:T(512)S(1)} %eq.52), kind=kOutput, calls=%fused_computation.64 | convolution fusion | flops 1612709888 | bytes 6817792 | tf_op jit(solution)/shard_map/dot_general | solution.py:71
  14.9 1.9 broadcast_in_dim.21
  16.8 289.8 %while.17 = (s32[]{:T(128)}, bf16[256,1536]{1,0:T(8,128)(2,1)}, bf16[4,256,1536]{2,1,0:T(8,128)(2,1)}, pred[]{:T(512)}, bf16[4,256,1536]{2,1,0:T(8,128)(2,1)}, /...) while((s32[]{:T(128)}, bf16[256,1536]{1,0:T(8,128)(2,1)}, ...), condition=%wide.region_2.3_spmd.clone, body=%wide.region_0.2_spmd.clone.sunk | while | flops 1252002048 | bytes 29496644 | solution.py:105
  19.9 3.0 collective-permute-start.1
  24.1 5.4 %fusion.50 = bf16[256,1536]{1,0:T(8,128)(2,1)} fusion(bf16[256,1536]{1,0:T(8,128)(2,1)S(1)} %get-tuple-element.339, bf16[1536,1536]{1,0:T(8,128)(2,1)} %get-tuple-element.409, bf16[256,1536]{1,0:T(8,128)(2,1)S(1)} %fusion.48, bf16[2,1536]{1,0:T(2,128)(2,1)S(1)} %collective-permute-done, bf16[2,1536]{1,0:T(2,128)(2,1)S(1)} %collective-permute-done.1, ...), kind=kOutput, calls=%fused_computation.10.clone.1 | convolution fusion | flops 1222901760 | bytes 7120896 | tf_op jit(solution)/shard_map/while/body/eval_jaxpr/dot_general | solution.py:55
  32.5 2.5 collective-permute-start.3
  36.3 4.6 %collective-permute-start.2 = (bf16[256,1536]{1,0:T(8,128)(2,1)}, bf16[256,1536]{1,0:T(8,128)(2,1)}, u32[]{:S(2)}, u32[]{:S(2)}) collective-permute-start(bf16[256,1536]{1,0:T(8,128)(2,1)} %fusion.50), channel_id=1, source_target_pairs={{0,8},{8,16},{16,24},{1,9},{9,17},{17,25},{2,10},{10,18},{18,26},{... | collective-permute-start | bytes 2359304 | tf_op jit(solution)/shard_map/while/body/eval_jaxpr/ppermute | solution.py:41
  40.9 2.4 collective-permute-start.4
  43.3 2.7 collective-permute-start.6
  47.1 2.3 collective-permute-start.8
  49.5 1.7 collective-permute-start.9
  51.2 4.6 %collective-permute-done.7 = bf16[32,1536]{1,0:T(8,128)(2,1)S(1)} collective-permute-done((bf16[32,1536]{1,0:T(8,128)(2,1)S(1)}, bf16[32,1536]{1,0:T(8,128)(2,1)S(1)}, u32[]{:S(2)}, u32[]{:S(2)}) %collective-permute-start.7) | collective-permute-done | bytes 98336 | tf_op jit(solution)/shard_map/while/body/eval_jaxpr/ppermute | solution.py:20
  60.4 3.0 collective-permute-start.1
  64.6 5.4 %fusion.50 = bf16[256,1536]{1,0:T(8,128)(2,1)} fusion(bf16[256,1536]{1,0:T(8,128)(2,1)S(1)} %get-tuple-element.339, bf16[1536,1536]{1,0:T(8,128)(2,1)} %get-tuple-element.409, bf16[256,1536]{1,0:T(8,128)(2,1)S(1)} %fusion.48, bf16[2,1536]{1,0:T(2,128)(2,1)S(1)} %collective-permute-done, bf16[2,1536]{1,0:T(2,128)(2,1)S(1)} %collective-permute-done.1, ...), kind=kOutput, calls=%fused_computation.10.clone.1 | convolution fusion | flops 1222901760 | bytes 7120896 | tf_op jit(solution)/shard_map/while/body/eval_jaxpr/dot_general | solution.py:55
  73.0 2.0 collective-permute-start.3
  76.2 5.5 %collective-permute-start.2 = (bf16[256,1536]{1,0:T(8,128)(2,1)}, bf16[256,1536]{1,0:T(8,128)(2,1)}, u32[]{:S(2)}, u32[]{:S(2)}) collective-permute-start(bf16[256,1536]{1,0:T(8,128)(2,1)} %fusion.50), channel_id=1, source_target_pairs={{0,8},{8,16},{16,24},{1,9},{9,17},{17,25},{2,10},{10,18},{18,26},{... | collective-permute-start | bytes 2359304 | tf_op jit(solution)/shard_map/while/body/eval_jaxpr/ppermute | solution.py:41
  81.7 3.1 %collective-permute-start.4 = (bf16[32,1536]{1,0:T(8,128)(2,1)}, bf16[32,1536]{1,0:T(8,128)(2,1)S(1)}, u32[]{:S(2)}, u32[]{:S(2)}) collective-permute-start(bf16[32,1536]{1,0:T(8,128)(2,1)} %get-tuple-element.350), channel_id=1, source_target_pairs={{0,2},{1,3},{2,0},{3,1},{4,6},{5,7},{6,4},{7,5},{8,10},{9,11},{10,... | collective-permute-start | bytes 294920 | tf_op jit(solution)/shard_map/while/body/eval_jaxpr/ppermute | solution.py:20
  84.9 2.7 collective-permute-start.6
  88.8 2.6 collective-permute-start.8
  91.4 1.5 collective-permute-start.9
  93.0 4.4 %collective-permute-done.7 = bf16[32,1536]{1,0:T(8,128)(2,1)S(1)} collective-permute-done((bf16[32,1536]{1,0:T(8,128)(2,1)S(1)}, bf16[32,1536]{1,0:T(8,128)(2,1)S(1)}, u32[]{:S(2)}, u32[]{:S(2)}) %collective-permute-start.7) | collective-permute-done | bytes 98336 | tf_op jit(solution)/shard_map/while/body/eval_jaxpr/ppermute | solution.py:20
  101.6 3.0 collective-permute-start.1
  105.9 5.4 %fusion.50 = bf16[256,1536]{1,0:T(8,128)(2,1)} fusion(bf16[256,1536]{1,0:T(8,128)(2,1)S(1)} %get-tuple-element.339, bf16[1536,1536]{1,0:T(8,128)(2,1)} %get-tuple-element.409, bf16[256,1536]{1,0:T(8,128)(2,1)S(1)} %fusion.48, bf16[2,1536]{1,0:T(2,128)(2,1)S(1)} %collective-permute-done, bf16[2,1536]{1,0:T(2,128)(2,1)S(1)} %collective-permute-done.1, ...), kind=kOutput, calls=%fused_computation.10.clone.1 | convolution fusion | flops 1222901760 | bytes 7120896 | tf_op jit(solution)/shard_map/while/body/eval_jaxpr/dot_general | solution.py:55
  114.3 2.4 collective-permute-start.3
  117.8 5.5 %collective-permute-start.2 = (bf16[256,1536]{1,0:T(8,128)(2,1)}, bf16[256,1536]{1,0:T(8,128)(2,1)}, u32[]{:S(2)}, u32[]{:S(2)}) collective-permute-start(bf16[256,1536]{1,0:T(8,128)(2,1)} %fusion.50), channel_id=1, source_target_pairs={{0,8},{8,16},{16,24},{1,9},{9,17},{17,25},{2,10},{10,18},{18,26},{... | collective-permute-start | bytes 2359304 | tf_op jit(solution)/shard_map/while/body/eval_jaxpr/ppermute | solution.py:41
  123.4 3.1 %collective-permute-start.4 = (bf16[32,1536]{1,0:T(8,128)(2,1)}, bf16[32,1536]{1,0:T(8,128)(2,1)S(1)}, u32[]{:S(2)}, u32[]{:S(2)}) collective-permute-start(bf16[32,1536]{1,0:T(8,128)(2,1)} %get-tuple-element.350), channel_id=1, source_target_pairs={{0,2},{1,3},{2,0},{3,1},{4,6},{5,7},{6,4},{7,5},{8,10},{9,11},{10,... | collective-permute-start | bytes 294920 | tf_op jit(solution)/shard_map/while/body/eval_jaxpr/ppermute | solution.py:20
  126.5 2.7 collective-permute-start.6
  130.4 2.6 collective-permute-start.8
  134.6 4.4 %collective-permute-done.7 = bf16[32,1536]{1,0:T(8,128)(2,1)S(1)} collective-permute-done((bf16[32,1536]{1,0:T(8,128)(2,1)S(1)}, bf16[32,1536]{1,0:T(8,128)(2,1)S(1)}, u32[]{:S(2)}, u32[]{:S(2)}) %collective-permute-start.7) | collective-permute-done | bytes 98336 | tf_op jit(solution)/shard_map/while/body/eval_jaxpr/ppermute | solution.py:20
  143.3 3.0 collective-permute-start.1
  147.5 5.4 %fusion.50 = bf16[256,1536]{1,0:T(8,128)(2,1)} fusion(bf16[256,1536]{1,0:T(8,128)(2,1)S(1)} %get-tuple-element.339, bf16[1536,1536]{1,0:T(8,128)(2,1)} %get-tuple-element.409, bf16[256,1536]{1,0:T(8,128)(2,1)S(1)} %fusion.48, bf16[2,1536]{1,0:T(2,128)(2,1)S(1)} %collective-permute-done, bf16[2,1536]{1,0:T(2,128)(2,1)S(1)} %collective-permute-done.1, ...), kind=kOutput, calls=%fused_computation.10.clone.1 | convolution fusion | flops 1222901760 | bytes 7120896 | tf_op jit(solution)/shard_map/while/body/eval_jaxpr/dot_general | solution.py:55
  155.9 2.4 collective-permute-start.3
  159.5 5.5 %collective-permute-start.2 = (bf16[256,1536]{1,0:T(8,128)(2,1)}, bf16[256,1536]{1,0:T(8,128)(2,1)}, u32[]{:S(2)}, u32[]{:S(2)}) collective-permute-start(bf16[256,1536]{1,0:T(8,128)(2,1)} %fusion.50), channel_id=1, source_target_pairs={{0,8},{8,16},{16,24},{1,9},{9,17},{17,25},{2,10},{10,18},{18,26},{... | collective-permute-start | bytes 2359304 | tf_op jit(solution)/shard_map/while/body/eval_jaxpr/ppermute | solution.py:41
  165.0 3.1 %collective-permute-start.4 = (bf16[32,1536]{1,0:T(8,128)(2,1)}, bf16[32,1536]{1,0:T(8,128)(2,1)S(1)}, u32[]{:S(2)}, u32[]{:S(2)}) collective-permute-start(bf16[32,1536]{1,0:T(8,128)(2,1)} %get-tuple-element.350), channel_id=1, source_target_pairs={{0,2},{1,3},{2,0},{3,1},{4,6},{5,7},{6,4},{7,5},{8,10},{9,11},{10,... | collective-permute-start | bytes 294920 | tf_op jit(solution)/shard_map/while/body/eval_jaxpr/ppermute | solution.py:20
  168.1 2.7 collective-permute-start.6
  172.0 2.6 collective-permute-start.8
  176.2 4.4 %collective-permute-done.7 = bf16[32,1536]{1,0:T(8,128)(2,1)S(1)} collective-permute-done((bf16[32,1536]{1,0:T(8,128)(2,1)S(1)}, bf16[32,1536]{1,0:T(8,128)(2,1)S(1)}, u32[]{:S(2)}, u32[]{:S(2)}) %collective-permute-start.7) | collective-permute-done | bytes 98336 | tf_op jit(solution)/shard_map/while/body/eval_jaxpr/ppermute | solution.py:20
  184.9 3.0 collective-permute-start.1
  189.1 5.4 %fusion.50 = bf16[256,1536]{1,0:T(8,128)(2,1)} fusion(bf16[256,1536]{1,0:T(8,128)(2,1)S(1)} %get-tuple-element.339, bf16[1536,1536]{1,0:T(8,128)(2,1)} %get-tuple-element.409, bf16[256,1536]{1,0:T(8,128)(2,1)S(1)} %fusion.48, bf16[2,1536]{1,0:T(2,128)(2,1)S(1)} %collective-permute-done, bf16[2,1536]{1,0:T(2,128)(2,1)S(1)} %collective-permute-done.1, ...), kind=kOutput, calls=%fused_computation.10.clone.1 | convolution fusion | flops 1222901760 | bytes 7120896 | tf_op jit(solution)/shard_map/while/body/eval_jaxpr/dot_general | solution.py:55
  197.5 2.4 collective-permute-start.3
  201.1 5.5 %collective-permute-start.2 = (bf16[256,1536]{1,0:T(8,128)(2,1)}, bf16[256,1536]{1,0:T(8,128)(2,1)}, u32[]{:S(2)}, u32[]{:S(2)}) collective-permute-start(bf16[256,1536]{1,0:T(8,128)(2,1)} %fusion.50), channel_id=1, source_target_pairs={{0,8},{8,16},{16,24},{1,9},{9,17},{17,25},{2,10},{10,18},{18,26},{... | collective-permute-start | bytes 2359304 | tf_op jit(solution)/shard_map/while/body/eval_jaxpr/ppermute | solution.py:41
  206.6 3.1 %collective-permute-start.4 = (bf16[32,1536]{1,0:T(8,128)(2,1)}, bf16[32,1536]{1,0:T(8,128)(2,1)S(1)}, u32[]{:S(2)}, u32[]{:S(2)}) collective-permute-start(bf16[32,1536]{1,0:T(8,128)(2,1)} %get-tuple-element.350), channel_id=1, source_target_pairs={{0,2},{1,3},{2,0},{3,1},{4,6},{5,7},{6,4},{7,5},{8,10},{9,11},{10,... | collective-permute-start | bytes 294920 | tf_op jit(solution)/shard_map/while/body/eval_jaxpr/ppermute | solution.py:20
  209.7 2.7 collective-permute-start.6
  213.6 2.6 collective-permute-start.8
  217.8 4.4 %collective-permute-done.7 = bf16[32,1536]{1,0:T(8,128)(2,1)S(1)} collective-permute-done((bf16[32,1536]{1,0:T(8,128)(2,1)S(1)}, bf16[32,1536]{1,0:T(8,128)(2,1)S(1)}, u32[]{:S(2)}, u32[]{:S(2)}) %collective-permute-start.7) | collective-permute-done | bytes 98336 | tf_op jit(solution)/shard_map/while/body/eval_jaxpr/ppermute | solution.py:20
  226.5 3.0 collective-permute-start.1
  230.7 5.4 %fusion.50 = bf16[256,1536]{1,0:T(8,128)(2,1)} fusion(bf16[256,1536]{1,0:T(8,128)(2,1)S(1)} %get-tuple-element.339, bf16[1536,1536]{1,0:T(8,128)(2,1)} %get-tuple-element.409, bf16[256,1536]{1,0:T(8,128)(2,1)S(1)} %fusion.48, bf16[2,1536]{1,0:T(2,128)(2,1)S(1)} %collective-permute-done, bf16[2,1536]{1,0:T(2,128)(2,1)S(1)} %collective-permute-done.1, ...), kind=kOutput, calls=%fused_computation.10.clone.1 | convolution fusion | flops 1222901760 | bytes 7120896 | tf_op jit(solution)/shard_map/while/body/eval_jaxpr/dot_general | solution.py:55
  239.1 2.4 collective-permute-start.3
  242.7 5.5 %collective-permute-start.2 = (bf16[256,1536]{1,0:T(8,128)(2,1)}, bf16[256,1536]{1,0:T(8,128)(2,1)}, u32[]{:S(2)}, u32[]{:S(2)}) collective-permute-start(bf16[256,1536]{1,0:T(8,128)(2,1)} %fusion.50), channel_id=1, source_target_pairs={{0,8},{8,16},{16,24},{1,9},{9,17},{17,25},{2,10},{10,18},{18,26},{... | collective-permute-start | bytes 2359304 | tf_op jit(solution)/shard_map/while/body/eval_jaxpr/ppermute | solution.py:41
  248.2 3.1 %collective-permute-start.4 = (bf16[32,1536]{1,0:T(8,128)(2,1)}, bf16[32,1536]{1,0:T(8,128)(2,1)S(1)}, u32[]{:S(2)}, u32[]{:S(2)}) collective-permute-start(bf16[32,1536]{1,0:T(8,128)(2,1)} %get-tuple-element.350), channel_id=1, source_target_pairs={{0,2},{1,3},{2,0},{3,1},{4,6},{5,7},{6,4},{7,5},{8,10},{9,11},{10,... | collective-permute-start | bytes 294920 | tf_op jit(solution)/shard_map/while/body/eval_jaxpr/ppermute | solution.py:20
  251.4 2.7 collective-permute-start.6
  255.2 2.6 collective-permute-start.8
  259.4 4.4 %collective-permute-done.7 = bf16[32,1536]{1,0:T(8,128)(2,1)S(1)} collective-permute-done((bf16[32,1536]{1,0:T(8,128)(2,1)S(1)}, bf16[32,1536]{1,0:T(8,128)(2,1)S(1)}, u32[]{:S(2)}, u32[]{:S(2)}) %collective-permute-start.7) | collective-permute-done | bytes 98336 | tf_op jit(solution)/shard_map/while/body/eval_jaxpr/ppermute | solution.py:20
  268.1 3.0 collective-permute-start.1
  272.3 5.4 %fusion.50 = bf16[256,1536]{1,0:T(8,128)(2,1)} fusion(bf16[256,1536]{1,0:T(8,128)(2,1)S(1)} %get-tuple-element.339, bf16[1536,1536]{1,0:T(8,128)(2,1)} %get-tuple-element.409, bf16[256,1536]{1,0:T(8,128)(2,1)S(1)} %fusion.48, bf16[2,1536]{1,0:T(2,128)(2,1)S(1)} %collective-permute-done, bf16[2,1536]{1,0:T(2,128)(2,1)S(1)} %collective-permute-done.1, ...), kind=kOutput, calls=%fused_computation.10.clone.1 | convolution fusion | flops 1222901760 | bytes 7120896 | tf_op jit(solution)/shard_map/while/body/eval_jaxpr/dot_general | solution.py:55
  280.7 2.4 collective-permute-start.3
  284.3 5.5 %collective-permute-start.2 = (bf16[256,1536]{1,0:T(8,128)(2,1)}, bf16[256,1536]{1,0:T(8,128)(2,1)}, u32[]{:S(2)}, u32[]{:S(2)}) collective-permute-start(bf16[256,1536]{1,0:T(8,128)(2,1)} %fusion.50), channel_id=1, source_target_pairs={{0,8},{8,16},{16,24},{1,9},{9,17},{17,25},{2,10},{10,18},{18,26},{... | collective-permute-start | bytes 2359304 | tf_op jit(solution)/shard_map/while/body/eval_jaxpr/ppermute | solution.py:41
  289.8 3.1 %collective-permute-start.4 = (bf16[32,1536]{1,0:T(8,128)(2,1)}, bf16[32,1536]{1,0:T(8,128)(2,1)S(1)}, u32[]{:S(2)}, u32[]{:S(2)}) collective-permute-start(bf16[32,1536]{1,0:T(8,128)(2,1)} %get-tuple-element.350), channel_id=1, source_target_pairs={{0,2},{1,3},{2,0},{3,1},{4,6},{5,7},{6,4},{7,5},{8,10},{9,11},{10,... | collective-permute-start | bytes 294920 | tf_op jit(solution)/shard_map/while/body/eval_jaxpr/ppermute | solution.py:20
  293.0 2.7 collective-permute-start.6
  296.8 2.6 collective-permute-start.8
  299.5 1.5 collective-permute-start.9
  301.0 4.4 %collective-permute-done.7 = bf16[32,1536]{1,0:T(8,128)(2,1)S(1)} collective-permute-done((bf16[32,1536]{1,0:T(8,128)(2,1)S(1)}, bf16[32,1536]{1,0:T(8,128)(2,1)S(1)}, u32[]{:S(2)}, u32[]{:S(2)}) %collective-permute-start.7) | collective-permute-done | bytes 98336 | tf_op jit(solution)/shard_map/while/body/eval_jaxpr/ppermute | solution.py:20
  (239 shorter events, 85.7 us)
Async XLA Ops:
  18.6 5.5 %collective-permute-start = (bf16[2,1536]{1,0:T(2,128)(2,1)S(1)}, bf16[2,1536]{1,0:T(2,128)(2,1)S(1)}, u32[]{:S(2)}, u32[]{:S(2)}) collective-permute-start(bf16[2,1536]{1,0:T(2,128)(2,1)S(1)} %get-tuple-element.341), channel_id=1, source_target_pairs={{1,0},{2,1},{3,2},{4,3},{5,4},{6,5},{7,6},{9,8},{10,9},{11,10},{12... | collective-permute-start | bytes 18440 | tf_op jit(solution)/shard_map/while/body/eval_jaxpr/ppermute | solution.py:33
  19.9 4.2 %collective-permute-start.1 = (bf16[2,1536]{1,0:T(2,128)(2,1)S(1)}, bf16[2,1536]{1,0:T(2,128)(2,1)S(1)}, u32[]{:S(2)}, u32[]{:S(2)}) collective-permute-start(bf16[2,1536]{1,0:T(2,128)(2,1)S(1)} %get-tuple-element.342), channel_id=1, source_target_pairs={{0,1},{1,2},{2,3},{3,4},{4,5},{5,6},{6,7},{8,9},{9,10},{10,11},{11... | collective-permute-start | bytes 18440 | tf_op jit(solution)/shard_map/while/body/eval_jaxpr/ppermute | solution.py:30
  32.5 13.5 %collective-permute-start.3 = (bf16[32,1536]{1,0:T(8,128)(2,1)}, bf16[32,1536]{1,0:T(8,128)(2,1)}, u32[]{:S(2)}, u32[]{:S(2)}) collective-permute-start(bf16[32,1536]{1,0:T(8,128)(2,1)} %get-tuple-element.349), channel_id=1, source_target_pairs={{0,1},{1,0},{2,3},{3,2},{4,5},{5,4},{6,7},{7,6},{8,9},{9,8},{10,11... | collective-permute-start | bytes 294920 | tf_op jit(solution)/shard_map/while/body/eval_jaxpr/ppermute | solution.py:20
  36.3 21.0 %collective-permute-start.2 = (bf16[256,1536]{1,0:T(8,128)(2,1)}, bf16[256,1536]{1,0:T(8,128)(2,1)}, u32[]{:S(2)}, u32[]{:S(2)}) collective-permute-start(bf16[256,1536]{1,0:T(8,128)(2,1)} %fusion.50), channel_id=1, source_target_pairs={{0,8},{8,16},{16,24},{1,9},{9,17},{17,25},{2,10},{10,18},{18,26},{... | collective-permute-start | bytes 2359304 | tf_op jit(solution)/shard_map/while/body/eval_jaxpr/ppermute | solution.py:41
  40.9 6.2 %collective-permute-start.4 = (bf16[32,1536]{1,0:T(8,128)(2,1)}, bf16[32,1536]{1,0:T(8,128)(2,1)S(1)}, u32[]{:S(2)}, u32[]{:S(2)}) collective-permute-start(bf16[32,1536]{1,0:T(8,128)(2,1)} %get-tuple-element.350), channel_id=1, source_target_pairs={{0,2},{1,3},{2,0},{3,1},{4,6},{5,7},{6,4},{7,5},{8,10},{9,11},{10,... | collective-permute-start | bytes 294920 | tf_op jit(solution)/shard_map/while/body/eval_jaxpr/ppermute | solution.py:20
  43.3 6.2 %collective-permute-start.5 = (bf16[32,1536]{1,0:T(8,128)(2,1)}, bf16[32,1536]{1,0:T(8,128)(2,1)S(1)}, u32[]{:S(2)}, u32[]{:S(2)}) collective-permute-start(bf16[32,1536]{1,0:T(8,128)(2,1)} %get-tuple-element.351), channel_id=1, source_target_pairs={{0,3},{1,2},{2,1},{3,0},{4,7},{5,6},{6,5},{7,4},{8,11},{9,10},{10,... | collective-permute-start | bytes 294920 | tf_op jit(solution)/shard_map/while/body/eval_jaxpr/ppermute | solution.py:20
  43.3 7.9 %collective-permute-start.6 = (bf16[32,1536]{1,0:T(8,128)(2,1)S(1)}, bf16[32,1536]{1,0:T(8,128)(2,1)S(1)}, u32[]{:S(2)}, u32[]{:S(2)}) collective-permute-start(bf16[32,1536]{1,0:T(8,128)(2,1)S(1)} %get-tuple-element.352), channel_id=1, source_target_pairs={{0,4},{1,5},{2,6},{3,7},{4,0},{5,1},{6,2},{7,3},{8,12},{9,13},{10,... | collective-permute-start | bytes 294920 | tf_op jit(solution)/shard_map/while/body/eval_jaxpr/ppermute | solution.py:20
  46.0 9.7 %collective-permute-start.7 = (bf16[32,1536]{1,0:T(8,128)(2,1)S(1)}, bf16[32,1536]{1,0:T(8,128)(2,1)S(1)}, u32[]{:S(2)}, u32[]{:S(2)}) collective-permute-start(bf16[32,1536]{1,0:T(8,128)(2,1)S(1)} %get-tuple-element.353), channel_id=1, source_target_pairs={{0,5},{1,4},{2,7},{3,6},{4,1},{5,0},{6,3},{7,2},{8,13},{9,12},{10,... | collective-permute-start | bytes 294920 | tf_op jit(solution)/shard_map/while/body/eval_jaxpr/ppermute | solution.py:20
  47.1 8.6 %collective-permute-start.8 = (bf16[32,1536]{1,0:T(8,128)(2,1)S(1)}, bf16[32,1536]{1,0:T(8,128)(2,1)S(1)}, u32[]{:S(2)}, u32[]{:S(2)}) collective-permute-start(bf16[32,1536]{1,0:T(8,128)(2,1)S(1)} %get-tuple-element.354), channel_id=1, source_target_pairs={{0,6},{1,7},{2,4},{3,5},{4,2},{5,3},{6,0},{7,1},{8,14},{9,15},{10,... | collective-permute-start | bytes 294920 | tf_op jit(solution)/shard_map/while/body/eval_jaxpr/ppermute | solution.py:20
  49.5 6.3 %collective-permute-start.9 = (bf16[32,1536]{1,0:T(8,128)(2,1)S(1)}, bf16[32,1536]{1,0:T(8,128)(2,1)S(1)}, u32[]{:S(2)}, u32[]{:S(2)}) collective-permute-start(bf16[32,1536]{1,0:T(8,128)(2,1)S(1)} %get-tuple-element.355), channel_id=1, source_target_pairs={{0,7},{1,6},{2,5},{3,4},{4,3},{5,2},{6,1},{7,0},{8,15},{9,14},{10,... | collective-permute-start | bytes 294920 | tf_op jit(solution)/shard_map/while/body/eval_jaxpr/ppermute | solution.py:20
  59.1 5.5 %collective-permute-start = (bf16[2,1536]{1,0:T(2,128)(2,1)S(1)}, bf16[2,1536]{1,0:T(2,128)(2,1)S(1)}, u32[]{:S(2)}, u32[]{:S(2)}) collective-permute-start(bf16[2,1536]{1,0:T(2,128)(2,1)S(1)} %get-tuple-element.341), channel_id=1, source_target_pairs={{1,0},{2,1},{3,2},{4,3},{5,4},{6,5},{7,6},{9,8},{10,9},{11,10},{12... | collective-permute-start | bytes 18440 | tf_op jit(solution)/shard_map/while/body/eval_jaxpr/ppermute | solution.py:33
  73.0 14.6 %collective-permute-start.3 = (bf16[32,1536]{1,0:T(8,128)(2,1)}, bf16[32,1536]{1,0:T(8,128)(2,1)}, u32[]{:S(2)}, u32[]{:S(2)}) collective-permute-start(bf16[32,1536]{1,0:T(8,128)(2,1)} %get-tuple-element.349), channel_id=1, source_target_pairs={{0,1},{1,0},{2,3},{3,2},{4,5},{5,4},{6,7},{7,6},{8,9},{9,8},{10,11... | collective-permute-start | bytes 294920 | tf_op jit(solution)/shard_map/while/body/eval_jaxpr/ppermute | solution.py:20
  76.2 22.3 %collective-permute-start.2 = (bf16[256,1536]{1,0:T(8,128)(2,1)}, bf16[256,1536]{1,0:T(8,128)(2,1)}, u32[]{:S(2)}, u32[]{:S(2)}) collective-permute-start(bf16[256,1536]{1,0:T(8,128)(2,1)} %fusion.50), channel_id=1, source_target_pairs={{0,8},{8,16},{16,24},{1,9},{9,17},{17,25},{2,10},{10,18},{18,26},{... | collective-permute-start | bytes 2359304 | tf_op jit(solution)/shard_map/while/body/eval_jaxpr/ppermute | solution.py:41
  81.7 7.0 %collective-permute-start.4 = (bf16[32,1536]{1,0:T(8,128)(2,1)}, bf16[32,1536]{1,0:T(8,128)(2,1)S(1)}, u32[]{:S(2)}, u32[]{:S(2)}) collective-permute-start(bf16[32,1536]{1,0:T(8,128)(2,1)} %get-tuple-element.350), channel_id=1, source_target_pairs={{0,2},{1,3},{2,0},{3,1},{4,6},{5,7},{6,4},{7,5},{8,10},{9,11},{10,... | collective-permute-start | bytes 294920 | tf_op jit(solution)/shard_map/while/body/eval_jaxpr/ppermute | solution.py:20
  84.9 6.5 %collective-permute-start.5 = (bf16[32,1536]{1,0:T(8,128)(2,1)}, bf16[32,1536]{1,0:T(8,128)(2,1)S(1)}, u32[]{:S(2)}, u32[]{:S(2)}) collective-permute-start(bf16[32,1536]{1,0:T(8,128)(2,1)} %get-tuple-element.351), channel_id=1, source_target_pairs={{0,3},{1,2},{2,1},{3,0},{4,7},{5,6},{6,5},{7,4},{8,11},{9,10},{10,... | collective-permute-start | bytes 294920 | tf_op jit(solution)/shard_map/while/body/eval_jaxpr/ppermute | solution.py:20
  84.9 8.0 %collective-permute-start.6 = (bf16[32,1536]{1,0:T(8,128)(2,1)S(1)}, bf16[32,1536]{1,0:T(8,128)(2,1)S(1)}, u32[]{:S(2)}, u32[]{:S(2)}) collective-permute-start(bf16[32,1536]{1,0:T(8,128)(2,1)S(1)} %get-tuple-element.352), channel_id=1, source_target_pairs={{0,4},{1,5},{2,6},{3,7},{4,0},{5,1},{6,2},{7,3},{8,12},{9,13},{10,... | collective-permute-start | bytes 294920 | tf_op jit(solution)/shard_map/while/body/eval_jaxpr/ppermute | solution.py:20
  87.6 9.7 %collective-permute-start.7 = (bf16[32,1536]{1,0:T(8,128)(2,1)S(1)}, bf16[32,1536]{1,0:T(8,128)(2,1)S(1)}, u32[]{:S(2)}, u32[]{:S(2)}) collective-permute-start(bf16[32,1536]{1,0:T(8,128)(2,1)S(1)} %get-tuple-element.353), channel_id=1, source_target_pairs={{0,5},{1,4},{2,7},{3,6},{4,1},{5,0},{6,3},{7,2},{8,13},{9,12},{10,... | collective-permute-start | bytes 294920 | tf_op jit(solution)/shard_map/while/body/eval_jaxpr/ppermute | solution.py:20
  88.8 8.6 %collective-permute-start.8 = (bf16[32,1536]{1,0:T(8,128)(2,1)S(1)}, bf16[32,1536]{1,0:T(8,128)(2,1)S(1)}, u32[]{:S(2)}, u32[]{:S(2)}) collective-permute-start(bf16[32,1536]{1,0:T(8,128)(2,1)S(1)} %get-tuple-element.354), channel_id=1, source_target_pairs={{0,6},{1,7},{2,4},{3,5},{4,2},{5,3},{6,0},{7,1},{8,14},{9,15},{10,... | collective-permute-start | bytes 294920 | tf_op jit(solution)/shard_map/while/body/eval_jaxpr/ppermute | solution.py:20
  91.4 6.0 %collective-permute-start.9 = (bf16[32,1536]{1,0:T(8,128)(2,1)S(1)}, bf16[32,1536]{1,0:T(8,128)(2,1)S(1)}, u32[]{:S(2)}, u32[]{:S(2)}) collective-permute-start(bf16[32,1536]{1,0:T(8,128)(2,1)S(1)} %get-tuple-element.355), channel_id=1, source_target_pairs={{0,7},{1,6},{2,5},{3,4},{4,3},{5,2},{6,1},{7,0},{8,15},{9,14},{10,... | collective-permute-start | bytes 294920 | tf_op jit(solution)/shard_map/while/body/eval_jaxpr/ppermute | solution.py:20
  100.3 5.5 %collective-permute-start = (bf16[2,1536]{1,0:T(2,128)(2,1)S(1)}, bf16[2,1536]{1,0:T(2,128)(2,1)S(1)}, u32[]{:S(2)}, u32[]{:S(2)}) collective-permute-start(bf16[2,1536]{1,0:T(2,128)(2,1)S(1)} %get-tuple-element.341), channel_id=1, source_target_pairs={{1,0},{2,1},{3,2},{4,3},{5,4},{6,5},{7,6},{9,8},{10,9},{11,10},{12... | collective-permute-start | bytes 18440 | tf_op jit(solution)/shard_map/while/body/eval_jaxpr/ppermute | solution.py:33
  114.3 15.0 %collective-permute-start.3 = (bf16[32,1536]{1,0:T(8,128)(2,1)}, bf16[32,1536]{1,0:T(8,128)(2,1)}, u32[]{:S(2)}, u32[]{:S(2)}) collective-permute-start(bf16[32,1536]{1,0:T(8,128)(2,1)} %get-tuple-element.349), channel_id=1, source_target_pairs={{0,1},{1,0},{2,3},{3,2},{4,5},{5,4},{6,7},{7,6},{8,9},{9,8},{10,11... | collective-permute-start | bytes 294920 | tf_op jit(solution)/shard_map/while/body/eval_jaxpr/ppermute | solution.py:20
  117.8 22.3 %collective-permute-start.2 = (bf16[256,1536]{1,0:T(8,128)(2,1)}, bf16[256,1536]{1,0:T(8,128)(2,1)}, u32[]{:S(2)}, u32[]{:S(2)}) collective-permute-start(bf16[256,1536]{1,0:T(8,128)(2,1)} %fusion.50), channel_id=1, source_target_pairs={{0,8},{8,16},{16,24},{1,9},{9,17},{17,25},{2,10},{10,18},{18,26},{... | collective-permute-start | bytes 2359304 | tf_op jit(solution)/shard_map/while/body/eval_jaxpr/ppermute | solution.py:41
  123.4 7.0 %collective-permute-start.4 = (bf16[32,1536]{1,0:T(8,128)(2,1)}, bf16[32,1536]{1,0:T(8,128)(2,1)S(1)}, u32[]{:S(2)}, u32[]{:S(2)}) collective-permute-start(bf16[32,1536]{1,0:T(8,128)(2,1)} %get-tuple-element.350), channel_id=1, source_target_pairs={{0,2},{1,3},{2,0},{3,1},{4,6},{5,7},{6,4},{7,5},{8,10},{9,11},{10,... | collective-permute-start | bytes 294920 | tf_op jit(solution)/shard_map/while/body/eval_jaxpr/ppermute | solution.py:20
  126.5 6.5 %collective-permute-start.5 = (bf16[32,1536]{1,0:T(8,128)(2,1)}, bf16[32,1536]{1,0:T(8,128)(2,1)S(1)}, u32[]{:S(2)}, u32[]{:S(2)}) collective-permute-start(bf16[32,1536]{1,0:T(8,128)(2,1)} %get-tuple-element.351), channel_id=1, source_target_pairs={{0,3},{1,2},{2,1},{3,0},{4,7},{5,6},{6,5},{7,4},{8,11},{9,10},{10,... | collective-permute-start | bytes 294920 | tf_op jit(solution)/shard_map/while/body/eval_jaxpr/ppermute | solution.py:20
  126.5 8.0 %collective-permute-start.6 = (bf16[32,1536]{1,0:T(8,128)(2,1)S(1)}, bf16[32,1536]{1,0:T(8,128)(2,1)S(1)}, u32[]{:S(2)}, u32[]{:S(2)}) collective-permute-start(bf16[32,1536]{1,0:T(8,128)(2,1)S(1)} %get-tuple-element.352), channel_id=1, source_target_pairs={{0,4},{1,5},{2,6},{3,7},{4,0},{5,1},{6,2},{7,3},{8,12},{9,13},{10,... | collective-permute-start | bytes 294920 | tf_op jit(solution)/shard_map/while/body/eval_jaxpr/ppermute | solution.py:20
  129.3 9.7 %collective-permute-start.7 = (bf16[32,1536]{1,0:T(8,128)(2,1)S(1)}, bf16[32,1536]{1,0:T(8,128)(2,1)S(1)}, u32[]{:S(2)}, u32[]{:S(2)}) collective-permute-start(bf16[32,1536]{1,0:T(8,128)(2,1)S(1)} %get-tuple-element.353), channel_id=1, source_target_pairs={{0,5},{1,4},{2,7},{3,6},{4,1},{5,0},{6,3},{7,2},{8,13},{9,12},{10,... | collective-permute-start | bytes 294920 | tf_op jit(solution)/shard_map/while/body/eval_jaxpr/ppermute | solution.py:20
  130.4 8.6 %collective-permute-start.8 = (bf16[32,1536]{1,0:T(8,128)(2,1)S(1)}, bf16[32,1536]{1,0:T(8,128)(2,1)S(1)}, u32[]{:S(2)}, u32[]{:S(2)}) collective-permute-start(bf16[32,1536]{1,0:T(8,128)(2,1)S(1)} %get-tuple-element.354), channel_id=1, source_target_pairs={{0,6},{1,7},{2,4},{3,5},{4,2},{5,3},{6,0},{7,1},{8,14},{9,15},{10,... | collective-permute-start | bytes 294920 | tf_op jit(solution)/shard_map/while/body/eval_jaxpr/ppermute | solution.py:20
  133.0 6.0 %collective-permute-start.9 = (bf16[32,1536]{1,0:T(8,128)(2,1)S(1)}, bf16[32,1536]{1,0:T(8,128)(2,1)S(1)}, u32[]{:S(2)}, u32[]{:S(2)}) collective-permute-start(bf16[32,1536]{1,0:T(8,128)(2,1)S(1)} %get-tuple-element.355), channel_id=1, source_target_pairs={{0,7},{1,6},{2,5},{3,4},{4,3},{5,2},{6,1},{7,0},{8,15},{9,14},{10,... | collective-permute-start | bytes 294920 | tf_op jit(solution)/shard_map/while/body/eval_jaxpr/ppermute | solution.py:20
  142.0 5.5 %collective-permute-start = (bf16[2,1536]{1,0:T(2,128)(2,1)S(1)}, bf16[2,1536]{1,0:T(2,128)(2,1)S(1)}, u32[]{:S(2)}, u32[]{:S(2)}) collective-permute-start(bf16[2,1536]{1,0:T(2,128)(2,1)S(1)} %get-tuple-element.341), channel_id=1, source_target_pairs={{1,0},{2,1},{3,2},{4,3},{5,4},{6,5},{7,6},{9,8},{10,9},{11,10},{12... | collective-permute-start | bytes 18440 | tf_op jit(solution)/shard_map/while/body/eval_jaxpr/ppermute | solution.py:33
  155.9 15.0 %collective-permute-start.3 = (bf16[32,1536]{1,0:T(8,128)(2,1)}, bf16[32,1536]{1,0:T(8,128)(2,1)}, u32[]{:S(2)}, u32[]{:S(2)}) collective-permute-start(bf16[32,1536]{1,0:T(8,128)(2,1)} %get-tuple-element.349), channel_id=1, source_target_pairs={{0,1},{1,0},{2,3},{3,2},{4,5},{5,4},{6,7},{7,6},{8,9},{9,8},{10,11... | collective-permute-start | bytes 294920 | tf_op jit(solution)/shard_map/while/body/eval_jaxpr/ppermute | solution.py:20
  159.5 22.3 %collective-permute-start.2 = (bf16[256,1536]{1,0:T(8,128)(2,1)}, bf16[256,1536]{1,0:T(8,128)(2,1)}, u32[]{:S(2)}, u32[]{:S(2)}) collective-permute-start(bf16[256,1536]{1,0:T(8,128)(2,1)} %fusion.50), channel_id=1, source_target_pairs={{0,8},{8,16},{16,24},{1,9},{9,17},{17,25},{2,10},{10,18},{18,26},{... | collective-permute-start | bytes 2359304 | tf_op jit(solution)/shard_map/while/body/eval_jaxpr/ppermute | solution.py:41
  165.0 7.0 %collective-permute-start.4 = (bf16[32,1536]{1,0:T(8,128)(2,1)}, bf16[32,1536]{1,0:T(8,128)(2,1)S(1)}, u32[]{:S(2)}, u32[]{:S(2)}) collective-permute-start(bf16[32,1536]{1,0:T(8,128)(2,1)} %get-tuple-element.350), channel_id=1, source_target_pairs={{0,2},{1,3},{2,0},{3,1},{4,6},{5,7},{6,4},{7,5},{8,10},{9,11},{10,... | collective-permute-start | bytes 294920 | tf_op jit(solution)/shard_map/while/body/eval_jaxpr/ppermute | solution.py:20
  168.1 6.5 %collective-permute-start.5 = (bf16[32,1536]{1,0:T(8,128)(2,1)}, bf16[32,1536]{1,0:T(8,128)(2,1)S(1)}, u32[]{:S(2)}, u32[]{:S(2)}) collective-permute-start(bf16[32,1536]{1,0:T(8,128)(2,1)} %get-tuple-element.351), channel_id=1, source_target_pairs={{0,3},{1,2},{2,1},{3,0},{4,7},{5,6},{6,5},{7,4},{8,11},{9,10},{10,... | collective-permute-start | bytes 294920 | tf_op jit(solution)/shard_map/while/body/eval_jaxpr/ppermute | solution.py:20
  168.1 8.0 %collective-permute-start.6 = (bf16[32,1536]{1,0:T(8,128)(2,1)S(1)}, bf16[32,1536]{1,0:T(8,128)(2,1)S(1)}, u32[]{:S(2)}, u32[]{:S(2)}) collective-permute-start(bf16[32,1536]{1,0:T(8,128)(2,1)S(1)} %get-tuple-element.352), channel_id=1, source_target_pairs={{0,4},{1,5},{2,6},{3,7},{4,0},{5,1},{6,2},{7,3},{8,12},{9,13},{10,... | collective-permute-start | bytes 294920 | tf_op jit(solution)/shard_map/while/body/eval_jaxpr/ppermute | solution.py:20
  170.9 9.7 %collective-permute-start.7 = (bf16[32,1536]{1,0:T(8,128)(2,1)S(1)}, bf16[32,1536]{1,0:T(8,128)(2,1)S(1)}, u32[]{:S(2)}, u32[]{:S(2)}) collective-permute-start(bf16[32,1536]{1,0:T(8,128)(2,1)S(1)} %get-tuple-element.353), channel_id=1, source_target_pairs={{0,5},{1,4},{2,7},{3,6},{4,1},{5,0},{6,3},{7,2},{8,13},{9,12},{10,... | collective-permute-start | bytes 294920 | tf_op jit(solution)/shard_map/while/body/eval_jaxpr/ppermute | solution.py:20
  172.0 8.6 %collective-permute-start.8 = (bf16[32,1536]{1,0:T(8,128)(2,1)S(1)}, bf16[32,1536]{1,0:T(8,128)(2,1)S(1)}, u32[]{:S(2)}, u32[]{:S(2)}) collective-permute-start(bf16[32,1536]{1,0:T(8,128)(2,1)S(1)} %get-tuple-element.354), channel_id=1, source_target_pairs={{0,6},{1,7},{2,4},{3,5},{4,2},{5,3},{6,0},{7,1},{8,14},{9,15},{10,... | collective-permute-start | bytes 294920 | tf_op jit(solution)/shard_map/while/body/eval_jaxpr/ppermute | solution.py:20
  174.6 6.0 %collective-permute-start.9 = (bf16[32,1536]{1,0:T(8,128)(2,1)S(1)}, bf16[32,1536]{1,0:T(8,128)(2,1)S(1)}, u32[]{:S(2)}, u32[]{:S(2)}) collective-permute-start(bf16[32,1536]{1,0:T(8,128)(2,1)S(1)} %get-tuple-element.355), channel_id=1, source_target_pairs={{0,7},{1,6},{2,5},{3,4},{4,3},{5,2},{6,1},{7,0},{8,15},{9,14},{10,... | collective-permute-start | bytes 294920 | tf_op jit(solution)/shard_map/while/body/eval_jaxpr/ppermute | solution.py:20
  183.6 5.5 %collective-permute-start = (bf16[2,1536]{1,0:T(2,128)(2,1)S(1)}, bf16[2,1536]{1,0:T(2,128)(2,1)S(1)}, u32[]{:S(2)}, u32[]{:S(2)}) collective-permute-start(bf16[2,1536]{1,0:T(2,128)(2,1)S(1)} %get-tuple-element.341), channel_id=1, source_target_pairs={{1,0},{2,1},{3,2},{4,3},{5,4},{6,5},{7,6},{9,8},{10,9},{11,10},{12... | collective-permute-start | bytes 18440 | tf_op jit(solution)/shard_map/while/body/eval_jaxpr/ppermute | solution.py:33
  197.5 15.0 %collective-permute-start.3 = (bf16[32,1536]{1,0:T(8,128)(2,1)}, bf16[32,1536]{1,0:T(8,128)(2,1)}, u32[]{:S(2)}, u32[]{:S(2)}) collective-permute-start(bf16[32,1536]{1,0:T(8,128)(2,1)} %get-tuple-element.349), channel_id=1, source_target_pairs={{0,1},{1,0},{2,3},{3,2},{4,5},{5,4},{6,7},{7,6},{8,9},{9,8},{10,11... | collective-permute-start | bytes 294920 | tf_op jit(solution)/shard_map/while/body/eval_jaxpr/ppermute | solution.py:20
  201.1 22.3 %collective-permute-start.2 = (bf16[256,1536]{1,0:T(8,128)(2,1)}, bf16[256,1536]{1,0:T(8,128)(2,1)}, u32[]{:S(2)}, u32[]{:S(2)}) collective-permute-start(bf16[256,1536]{1,0:T(8,128)(2,1)} %fusion.50), channel_id=1, source_target_pairs={{0,8},{8,16},{16,24},{1,9},{9,17},{17,25},{2,10},{10,18},{18,26},{... | collective-permute-start | bytes 2359304 | tf_op jit(solution)/shard_map/while/body/eval_jaxpr/ppermute | solution.py:41
  206.6 7.0 %collective-permute-start.4 = (bf16[32,1536]{1,0:T(8,128)(2,1)}, bf16[32,1536]{1,0:T(8,128)(2,1)S(1)}, u32[]{:S(2)}, u32[]{:S(2)}) collective-permute-start(bf16[32,1536]{1,0:T(8,128)(2,1)} %get-tuple-element.350), channel_id=1, source_target_pairs={{0,2},{1,3},{2,0},{3,1},{4,6},{5,7},{6,4},{7,5},{8,10},{9,11},{10,... | collective-permute-start | bytes 294920 | tf_op jit(solution)/shard_map/while/body/eval_jaxpr/ppermute | solution.py:20
  209.7 6.5 %collective-permute-start.5 = (bf16[32,1536]{1,0:T(8,128)(2,1)}, bf16[32,1536]{1,0:T(8,128)(2,1)S(1)}, u32[]{:S(2)}, u32[]{:S(2)}) collective-permute-start(bf16[32,1536]{1,0:T(8,128)(2,1)} %get-tuple-element.351), channel_id=1, source_target_pairs={{0,3},{1,2},{2,1},{3,0},{4,7},{5,6},{6,5},{7,4},{8,11},{9,10},{10,... | collective-permute-start | bytes 294920 | tf_op jit(solution)/shard_map/while/body/eval_jaxpr/ppermute | solution.py:20
  209.7 8.0 %collective-permute-start.6 = (bf16[32,1536]{1,0:T(8,128)(2,1)S(1)}, bf16[32,1536]{1,0:T(8,128)(2,1)S(1)}, u32[]{:S(2)}, u32[]{:S(2)}) collective-permute-start(bf16[32,1536]{1,0:T(8,128)(2,1)S(1)} %get-tuple-element.352), channel_id=1, source_target_pairs={{0,4},{1,5},{2,6},{3,7},{4,0},{5,1},{6,2},{7,3},{8,12},{9,13},{10,... | collective-permute-start | bytes 294920 | tf_op jit(solution)/shard_map/while/body/eval_jaxpr/ppermute | solution.py:20
  212.5 9.7 %collective-permute-start.7 = (bf16[32,1536]{1,0:T(8,128)(2,1)S(1)}, bf16[32,1536]{1,0:T(8,128)(2,1)S(1)}, u32[]{:S(2)}, u32[]{:S(2)}) collective-permute-start(bf16[32,1536]{1,0:T(8,128)(2,1)S(1)} %get-tuple-element.353), channel_id=1, source_target_pairs={{0,5},{1,4},{2,7},{3,6},{4,1},{5,0},{6,3},{7,2},{8,13},{9,12},{10,... | collective-permute-start | bytes 294920 | tf_op jit(solution)/shard_map/while/body/eval_jaxpr/ppermute | solution.py:20
  213.6 8.6 %collective-permute-start.8 = (bf16[32,1536]{1,0:T(8,128)(2,1)S(1)}, bf16[32,1536]{1,0:T(8,128)(2,1)S(1)}, u32[]{:S(2)}, u32[]{:S(2)}) collective-permute-start(bf16[32,1536]{1,0:T(8,128)(2,1)S(1)} %get-tuple-element.354), channel_id=1, source_target_pairs={{0,6},{1,7},{2,4},{3,5},{4,2},{5,3},{6,0},{7,1},{8,14},{9,15},{10,... | collective-permute-start | bytes 294920 | tf_op jit(solution)/shard_map/while/body/eval_jaxpr/ppermute | solution.py:20
  216.3 6.0 %collective-permute-start.9 = (bf16[32,1536]{1,0:T(8,128)(2,1)S(1)}, bf16[32,1536]{1,0:T(8,128)(2,1)S(1)}, u32[]{:S(2)}, u32[]{:S(2)}) collective-permute-start(bf16[32,1536]{1,0:T(8,128)(2,1)S(1)} %get-tuple-element.355), channel_id=1, source_target_pairs={{0,7},{1,6},{2,5},{3,4},{4,3},{5,2},{6,1},{7,0},{8,15},{9,14},{10,... | collective-permute-start | bytes 294920 | tf_op jit(solution)/shard_map/while/body/eval_jaxpr/ppermute | solution.py:20
  225.2 5.5 %collective-permute-start = (bf16[2,1536]{1,0:T(2,128)(2,1)S(1)}, bf16[2,1536]{1,0:T(2,128)(2,1)S(1)}, u32[]{:S(2)}, u32[]{:S(2)}) collective-permute-start(bf16[2,1536]{1,0:T(2,128)(2,1)S(1)} %get-tuple-element.341), channel_id=1, source_target_pairs={{1,0},{2,1},{3,2},{4,3},{5,4},{6,5},{7,6},{9,8},{10,9},{11,10},{12... | collective-permute-start | bytes 18440 | tf_op jit(solution)/shard_map/while/body/eval_jaxpr/ppermute | solution.py:33
  239.1 15.0 %collective-permute-start.3 = (bf16[32,1536]{1,0:T(8,128)(2,1)}, bf16[32,1536]{1,0:T(8,128)(2,1)}, u32[]{:S(2)}, u32[]{:S(2)}) collective-permute-start(bf16[32,1536]{1,0:T(8,128)(2,1)} %get-tuple-element.349), channel_id=1, source_target_pairs={{0,1},{1,0},{2,3},{3,2},{4,5},{5,4},{6,7},{7,6},{8,9},{9,8},{10,11... | collective-permute-start | bytes 294920 | tf_op jit(solution)/shard_map/while/body/eval_jaxpr/ppermute | solution.py:20
  242.7 22.3 %collective-permute-start.2 = (bf16[256,1536]{1,0:T(8,128)(2,1)}, bf16[256,1536]{1,0:T(8,128)(2,1)}, u32[]{:S(2)}, u32[]{:S(2)}) collective-permute-start(bf16[256,1536]{1,0:T(8,128)(2,1)} %fusion.50), channel_id=1, source_target_pairs={{0,8},{8,16},{16,24},{1,9},{9,17},{17,25},{2,10},{10,18},{18,26},{... | collective-permute-start | bytes 2359304 | tf_op jit(solution)/shard_map/while/body/eval_jaxpr/ppermute | solution.py:41
  248.2 7.0 %collective-permute-start.4 = (bf16[32,1536]{1,0:T(8,128)(2,1)}, bf16[32,1536]{1,0:T(8,128)(2,1)S(1)}, u32[]{:S(2)}, u32[]{:S(2)}) collective-permute-start(bf16[32,1536]{1,0:T(8,128)(2,1)} %get-tuple-element.350), channel_id=1, source_target_pairs={{0,2},{1,3},{2,0},{3,1},{4,6},{5,7},{6,4},{7,5},{8,10},{9,11},{10,... | collective-permute-start | bytes 294920 | tf_op jit(solution)/shard_map/while/body/eval_jaxpr/ppermute | solution.py:20
  251.3 6.5 %collective-permute-start.5 = (bf16[32,1536]{1,0:T(8,128)(2,1)}, bf16[32,1536]{1,0:T(8,128)(2,1)S(1)}, u32[]{:S(2)}, u32[]{:S(2)}) collective-permute-start(bf16[32,1536]{1,0:T(8,128)(2,1)} %get-tuple-element.351), channel_id=1, source_target_pairs={{0,3},{1,2},{2,1},{3,0},{4,7},{5,6},{6,5},{7,4},{8,11},{9,10},{10,... | collective-permute-start | bytes 294920 | tf_op jit(solution)/shard_map/while/body/eval_jaxpr/ppermute | solution.py:20
  251.4 8.0 %collective-permute-start.6 = (bf16[32,1536]{1,0:T(8,128)(2,1)S(1)}, bf16[32,1536]{1,0:T(8,128)(2,1)S(1)}, u32[]{:S(2)}, u32[]{:S(2)}) collective-permute-start(bf16[32,1536]{1,0:T(8,128)(2,1)S(1)} %get-tuple-element.352), channel_id=1, source_target_pairs={{0,4},{1,5},{2,6},{3,7},{4,0},{5,1},{6,2},{7,3},{8,12},{9,13},{10,... | collective-permute-start | bytes 294920 | tf_op jit(solution)/shard_map/while/body/eval_jaxpr/ppermute | solution.py:20
  254.1 9.7 %collective-permute-start.7 = (bf16[32,1536]{1,0:T(8,128)(2,1)S(1)}, bf16[32,1536]{1,0:T(8,128)(2,1)S(1)}, u32[]{:S(2)}, u32[]{:S(2)}) collective-permute-start(bf16[32,1536]{1,0:T(8,128)(2,1)S(1)} %get-tuple-element.353), channel_id=1, source_target_pairs={{0,5},{1,4},{2,7},{3,6},{4,1},{5,0},{6,3},{7,2},{8,13},{9,12},{10,... | collective-permute-start | bytes 294920 | tf_op jit(solution)/shard_map/while/body/eval_jaxpr/ppermute | solution.py:20
  255.2 8.6 %collective-permute-start.8 = (bf16[32,1536]{1,0:T(8,128)(2,1)S(1)}, bf16[32,1536]{1,0:T(8,128)(2,1)S(1)}, u32[]{:S(2)}, u32[]{:S(2)}) collective-permute-start(bf16[32,1536]{1,0:T(8,128)(2,1)S(1)} %get-tuple-element.354), channel_id=1, source_target_pairs={{0,6},{1,7},{2,4},{3,5},{4,2},{5,3},{6,0},{7,1},{8,14},{9,15},{10,... | collective-permute-start | bytes 294920 | tf_op jit(solution)/shard_map/while/body/eval_jaxpr/ppermute | solution.py:20
  257.9 6.0 %collective-permute-start.9 = (bf16[32,1536]{1,0:T(8,128)(2,1)S(1)}, bf16[32,1536]{1,0:T(8,128)(2,1)S(1)}, u32[]{:S(2)}, u32[]{:S(2)}) collective-permute-start(bf16[32,1536]{1,0:T(8,128)(2,1)S(1)} %get-tuple-element.355), channel_id=1, source_target_pairs={{0,7},{1,6},{2,5},{3,4},{4,3},{5,2},{6,1},{7,0},{8,15},{9,14},{10,... | collective-permute-start | bytes 294920 | tf_op jit(solution)/shard_map/while/body/eval_jaxpr/ppermute | solution.py:20
  266.8 5.5 %collective-permute-start = (bf16[2,1536]{1,0:T(2,128)(2,1)S(1)}, bf16[2,1536]{1,0:T(2,128)(2,1)S(1)}, u32[]{:S(2)}, u32[]{:S(2)}) collective-permute-start(bf16[2,1536]{1,0:T(2,128)(2,1)S(1)} %get-tuple-element.341), channel_id=1, source_target_pairs={{1,0},{2,1},{3,2},{4,3},{5,4},{6,5},{7,6},{9,8},{10,9},{11,10},{12... | collective-permute-start | bytes 18440 | tf_op jit(solution)/shard_map/while/body/eval_jaxpr/ppermute | solution.py:33
  280.7 15.0 %collective-permute-start.3 = (bf16[32,1536]{1,0:T(8,128)(2,1)}, bf16[32,1536]{1,0:T(8,128)(2,1)}, u32[]{:S(2)}, u32[]{:S(2)}) collective-permute-start(bf16[32,1536]{1,0:T(8,128)(2,1)} %get-tuple-element.349), channel_id=1, source_target_pairs={{0,1},{1,0},{2,3},{3,2},{4,5},{5,4},{6,7},{7,6},{8,9},{9,8},{10,11... | collective-permute-start | bytes 294920 | tf_op jit(solution)/shard_map/while/body/eval_jaxpr/ppermute | solution.py:20
  284.3 22.3 %collective-permute-start.2 = (bf16[256,1536]{1,0:T(8,128)(2,1)}, bf16[256,1536]{1,0:T(8,128)(2,1)}, u32[]{:S(2)}, u32[]{:S(2)}) collective-permute-start(bf16[256,1536]{1,0:T(8,128)(2,1)} %fusion.50), channel_id=1, source_target_pairs={{0,8},{8,16},{16,24},{1,9},{9,17},{17,25},{2,10},{10,18},{18,26},{... | collective-permute-start | bytes 2359304 | tf_op jit(solution)/shard_map/while/body/eval_jaxpr/ppermute | solution.py:41
  289.8 7.0 %collective-permute-start.4 = (bf16[32,1536]{1,0:T(8,128)(2,1)}, bf16[32,1536]{1,0:T(8,128)(2,1)S(1)}, u32[]{:S(2)}, u32[]{:S(2)}) collective-permute-start(bf16[32,1536]{1,0:T(8,128)(2,1)} %get-tuple-element.350), channel_id=1, source_target_pairs={{0,2},{1,3},{2,0},{3,1},{4,6},{5,7},{6,4},{7,5},{8,10},{9,11},{10,... | collective-permute-start | bytes 294920 | tf_op jit(solution)/shard_map/while/body/eval_jaxpr/ppermute | solution.py:20
  293.0 6.5 %collective-permute-start.5 = (bf16[32,1536]{1,0:T(8,128)(2,1)}, bf16[32,1536]{1,0:T(8,128)(2,1)S(1)}, u32[]{:S(2)}, u32[]{:S(2)}) collective-permute-start(bf16[32,1536]{1,0:T(8,128)(2,1)} %get-tuple-element.351), channel_id=1, source_target_pairs={{0,3},{1,2},{2,1},{3,0},{4,7},{5,6},{6,5},{7,4},{8,11},{9,10},{10,... | collective-permute-start | bytes 294920 | tf_op jit(solution)/shard_map/while/body/eval_jaxpr/ppermute | solution.py:20
  293.0 8.0 %collective-permute-start.6 = (bf16[32,1536]{1,0:T(8,128)(2,1)S(1)}, bf16[32,1536]{1,0:T(8,128)(2,1)S(1)}, u32[]{:S(2)}, u32[]{:S(2)}) collective-permute-start(bf16[32,1536]{1,0:T(8,128)(2,1)S(1)} %get-tuple-element.352), channel_id=1, source_target_pairs={{0,4},{1,5},{2,6},{3,7},{4,0},{5,1},{6,2},{7,3},{8,12},{9,13},{10,... | collective-permute-start | bytes 294920 | tf_op jit(solution)/shard_map/while/body/eval_jaxpr/ppermute | solution.py:20
  295.7 9.7 %collective-permute-start.7 = (bf16[32,1536]{1,0:T(8,128)(2,1)S(1)}, bf16[32,1536]{1,0:T(8,128)(2,1)S(1)}, u32[]{:S(2)}, u32[]{:S(2)}) collective-permute-start(bf16[32,1536]{1,0:T(8,128)(2,1)S(1)} %get-tuple-element.353), channel_id=1, source_target_pairs={{0,5},{1,4},{2,7},{3,6},{4,1},{5,0},{6,3},{7,2},{8,13},{9,12},{10,... | collective-permute-start | bytes 294920 | tf_op jit(solution)/shard_map/while/body/eval_jaxpr/ppermute | solution.py:20
  296.8 8.6 %collective-permute-start.8 = (bf16[32,1536]{1,0:T(8,128)(2,1)S(1)}, bf16[32,1536]{1,0:T(8,128)(2,1)S(1)}, u32[]{:S(2)}, u32[]{:S(2)}) collective-permute-start(bf16[32,1536]{1,0:T(8,128)(2,1)S(1)} %get-tuple-element.354), channel_id=1, source_target_pairs={{0,6},{1,7},{2,4},{3,5},{4,2},{5,3},{6,0},{7,1},{8,14},{9,15},{10,... | collective-permute-start | bytes 294920 | tf_op jit(solution)/shard_map/while/body/eval_jaxpr/ppermute | solution.py:20
  299.5 6.0 %collective-permute-start.9 = (bf16[32,1536]{1,0:T(8,128)(2,1)S(1)}, bf16[32,1536]{1,0:T(8,128)(2,1)S(1)}, u32[]{:S(2)}, u32[]{:S(2)}) collective-permute-start(bf16[32,1536]{1,0:T(8,128)(2,1)S(1)} %get-tuple-element.355), channel_id=1, source_target_pairs={{0,7},{1,6},{2,5},{3,4},{4,3},{5,2},{6,1},{7,0},{8,15},{9,14},{10,... | collective-permute-start | bytes 294920 | tf_op jit(solution)/shard_map/while/body/eval_jaxpr/ppermute | solution.py:20
  (8 other events, 35.9 us)
